TPU v7x, 512 devices: a whole 4x4x16 slice. The times are simulated.
512 devices in a mesh: row: 8 (over x, core), col: 16 (over z), depth: 4 (over y).
Axes of the slice: x: 4, y: 4, z: 16, core: 2. Of those that a mesh axis runs over, the one named last changes fastest.
Arguments:
- density: float32 [4096, 4096], P('row', 'col'), as said below
- pattern: int32 [32, 32], P('row', 'col'), may hold values from 0 to 1, as said below
- branch: int32 [4], replicated, may hold values from 0 to 1, as said below
Outputs:
- purified: float32 [4096, 4096], P('row', 'col')
Inputs may be any that keep to these rules, and one draw needn't show every extreme that they name: `branch`: each entry is 0 or 1; both values occur. Each entry is 0 or 1, and pattern[i, j] = pattern[j, i]. density is symmetric: density[i, j] = density[j, i].
All inputs are finite; a program needn't handle non-finite values.
Results may differ from a plain program's by a relative error of at most 0.00026.
Values sent between devices are 32-bit elements; how exact they have to be, the bound alone decides.
No kernel may reach another device: no remote copies, remote signals or barrier semaphores. Data moves between devices by JAX's collectives and lax.ppermute only.
A program may use at most 64 MiB of HBM per device.

v0:
```python
import functools

import jax
import jax.numpy as jnp
from jax import lax
from jax.experimental import pallas as pl
from jax.experimental.pallas import tpu as pltpu
from jax.sharding import PartitionSpec as P

TILE = 128
STEPS = 4
LANES = 8
NATURAL = 18
BALANCED = 14


def exchange(parts, axis, groups=None):
    return lax.all_to_all(parts, axis, 0, 0, axis_index_groups=groups, tiled=True)


def gather(part, axis, members, groups=None):
    return exchange(jnp.broadcast_to(part[None], (members,) + part.shape), axis, groups)


def shifted(parts, by):
    cols = lax.axis_size("col")
    return lax.ppermute(parts, "col", [(z, (z + by) % cols) for z in range(cols)])


def sum_along_col(ahead):
    cols = lax.axis_size("col")
    far = [[c + 4 * m for m in range(cols // 4)] for c in range(4)]
    near = ahead[0] + shifted(ahead[1], 1) + shifted(ahead[3], -1)
    near = near + jnp.concatenate([shifted(ahead[2][:2], 2), shifted(ahead[2][2:], -2)])
    return exchange(near, "col", far).sum(0)


def swap_cores(value):
    return lax.ppermute(value, "row", [(i, i ^ 1) for i in range(lax.axis_size("row"))])


def dense(density, pattern, branch):
    rows, cols = lax.axis_size("row"), lax.axis_size("col")
    layers = lax.axis_size("depth")
    row, col, layer = lax.axis_index("row"), lax.axis_index("col"), lax.axis_index("depth")
    height, width = density.shape
    sub = width // layers
    core = row % 2
    cores_apart = [[x * 2 + c for x in range(rows // 2)] for c in range(2)]

    row_ids = lax.broadcasted_iota(jnp.int32, pattern.shape, 0) + row * pattern.shape[0]
    col_ids = lax.broadcasted_iota(jnp.int32, pattern.shape, 1) + col * pattern.shape[1]
    tiles = jnp.where(row_ids == col_ids, 1, pattern).T.astype(jnp.float32)
    keep = jnp.repeat(jnp.repeat(tiles, TILE, axis=0), TILE, axis=1)
    keep_part = lax.dynamic_slice_in_dim(keep, layer * sub, sub, 0)

    panel = density.T * keep
    part = lax.dynamic_slice_in_dim(panel, layer * sub, sub, 0)
    for step in range(STEPS):
        mine = panel.T.reshape(height // width, layers, sub, width)
        mine = lax.dynamic_index_in_dim(mine, layer, 1, keepdims=False)
        own = gather(mine, "row", rows // 2, cores_apart)
        other = swap_cores(own)

        def product(left, panel=panel):
            out = jnp.dot(
                left.reshape(-1, width), panel, precision=lax.Precision.HIGH, preferred_element_type=jnp.float32
            )
            return out.reshape(rows // 2, 2, sub, height)

        both = jnp.stack([product(own), product(other)])

        def of_class(k, both=both):
            k = k % 4
            start = ((k // 2) ^ core, 0, k % 2, 0, 0)
            out = lax.dynamic_slice(both, start, (1, rows // 2, 1, sub, height))
            return out.reshape(rows // 2, sub, height)

        squared = sum_along_col([of_class(col + q) for q in range(4)])
        part = keep_part * jnp.where(branch[step] == 1, squared, 2.0 * part - squared)
        panel = gather(part, "depth", layers).reshape(width, height)
    return panel.T


def column_order(keep):
    n = keep.shape[0]
    load = keep.sum(0)
    ids = jnp.arange(n)
    ahead = (load[None, :] > load[:, None]) | ((load[None, :] == load[:, None]) & (ids[None, :] < ids[:, None]))
    rank = ahead.astype(jnp.int32).sum(1)
    place = jnp.where(rank < n // 2, 2 * rank, 2 * (n - 1 - rank) + 1)
    return jnp.where(place[None, :] == ids[:, None], ids[None, :], 0).sum(1)


def slot_list(held, columns, slots):
    n = held.shape[-1]
    ids = jnp.arange(n)
    upto = (ids[:, None] <= ids[None, :]).astype(jnp.float32)
    count = jnp.dot(held.astype(jnp.float32), upto).astype(jnp.int32)
    which = jnp.arange(2)[:, None]
    place = count - 1 + which * count[..., :1, -1:]
    value = 1 + 2 * n * (n * columns[..., None] + ids) + n * which + ids
    hit = (held > 0)[..., None] & (place[..., None] == jnp.arange(2 * slots))
    return jnp.where(hit, value[..., None], 0).sum((-3, -2))


def spot(packed, blocks, in_product):
    at = jnp.maximum(packed - 1, 0)
    at = at >> blocks.bit_length() if in_product else at & (2 * blocks - 1)
    return at >> (blocks.bit_length() - 1), pl.ds(pl.multiple_of((at & (blocks - 1)) * TILE, TILE), TILE)


def pick_kernel(info_ref, from_ref, out_ref, *, slots, blocks):
    for t in range(slots):
        block, lanes = spot(info_ref[t], blocks, False)
        rows = pl.ds(pl.multiple_of(block * LANES, LANES), LANES)
        out_ref[t * LANES : (t + 1) * LANES, :] = jnp.where(info_ref[t] > 0, from_ref[rows, lanes], 0.0)


def place_kernel(info_ref, own_ref, other_ref, out_ref, *, slots, blocks):
    out_ref[...] = jnp.zeros_like(out_ref)
    for base, ref in ((0, own_ref), (slots, other_ref)):
        for t in range(slots):
            block, lanes = spot(info_ref[base + t], blocks, False)

            @pl.when(info_ref[base + t] > 0)
            def _(block=block, lanes=lanes, ref=ref, t=t):
                rows = pl.ds(pl.multiple_of(block * LANES, LANES), LANES)
                out_ref[rows, lanes] = ref[t * LANES : (t + 1) * LANES, :]


def step_kernel(info_ref, own_ref, other_ref, out_ref, x_ref, hi_ref, lo_ref, left_ref, prod_ref,
                *, slots_in, slots_out, blocks):
    share, square = info_ref[0], info_ref[3]
    sharers = TILE // LANES
    x_ref[...] = jnp.zeros_like(x_ref)
    for base, ref in ((4, own_ref), (4 + slots_in, other_ref)):

        def place(t, _, base=base, ref=ref):
            block, lanes = spot(info_ref[base + t], blocks, False)

            @pl.when(info_ref[base + t] > 0)
            def _():
                rows = pl.ds(pl.multiple_of(t * LANES, LANES), LANES)
                for s in range(sharers):
                    at = pl.multiple_of(block * TILE + s * LANES, LANES)
                    x_ref[pl.ds(at, LANES), lanes] = ref[s, rows, :]

            return 0

        lax.fori_loop(0, slots_in, place, 0)

    group = lax.broadcasted_iota(jnp.int32, (x_ref.shape[0], TILE), 1) // LANES
    for j in range(blocks):
        lanes = slice(j * TILE, (j + 1) * TILE)
        x = x_ref[:, lanes]
        hi = x.astype(jnp.bfloat16)
        hi_ref[:, lanes] = hi
        lo_ref[:, lanes] = (x - hi.astype(jnp.float32)).astype(jnp.bfloat16)
        half = slice(j // sharers * TILE, (j // sharers + 1) * TILE)
        turned = pltpu.roll(x, ((j - share) & (sharers - 1)) * LANES, 1)
        left_ref[:, half] = jnp.where(group == j % sharers, turned, left_ref[:, half])
    left = left_ref[...].T
    a_hi = left.astype(jnp.bfloat16)
    a_lo = (left - a_hi.astype(jnp.float32)).astype(jnp.bfloat16)
    wide = 4 * TILE
    for j in range(blocks * TILE // wide):
        lanes = slice(j * wide, (j + 1) * wide)
        b_hi, b_lo = hi_ref[:, lanes], lo_ref[:, lanes]
        prod_ref[:, lanes] = (
            jnp.dot(a_hi, b_hi, preferred_element_type=jnp.float32)
            + jnp.dot(a_hi, b_lo, preferred_element_type=jnp.float32)
            + jnp.dot(a_lo, b_hi, preferred_element_type=jnp.float32)
        )

    sign = jnp.where(square == 1, 1.0, -1.0)
    weight = jnp.where(square == 1, 0.0, -2.0)
    for half in range(2):
        rows = pl.ds(pl.multiple_of(info_ref[1 + half] * LANES, LANES), LANES)
        mine = pl.ds(pl.multiple_of(half * TILE + share * LANES, LANES), LANES)
        prod_ref[rows, :] = prod_ref[rows, :] + weight * x_ref[mine, :]

    first = 4 + 2 * slots_in

    def pick(t, _):
        packed = info_ref[first + t]
        block, lanes = spot(packed, blocks, True)
        rows = pl.ds(pl.multiple_of(block * LANES, LANES), LANES)
        out = pl.ds(pl.multiple_of(t * LANES, LANES), LANES)
        out_ref[out, :] = jnp.where(packed > 0, sign * prod_ref[rows, lanes], 0.0)
        return 0

    lax.fori_loop(0, out_ref.shape[0] // LANES, pick, 0, unroll=8)


def on_core(kernel, shape, scratch=()):
    vmem_spec, smem_spec = pl.BlockSpec(memory_space=pltpu.VMEM), pl.BlockSpec(memory_space=pltpu.SMEM)

    def call(info, *arrays):
        return pl.pallas_call(
            kernel,
            out_shape=jax.ShapeDtypeStruct(shape, jnp.float32),
            in_specs=[smem_spec] + [vmem_spec] * len(arrays),
            out_specs=vmem_spec,
            scratch_shapes=list(scratch),
            compiler_params=pltpu.CompilerParams(vmem_limit_bytes=48 * 1024 * 1024),
        )(info, *arrays)

    return call


def plane_groups():
    rows, layers = lax.axis_size("row"), lax.axis_size("depth")
    return [[(x * 2 + c) * layers + y for x in range(rows // 2) for y in range(layers)] for c in range(2)]


def in_plane(part):
    own = gather(part, ("row", "depth"), TILE // LANES, plane_groups())
    return own, swap_cores(own)


def sparse(own, other, natural, balanced, order, branch):
    rows, cols, layers = lax.axis_size("row"), lax.axis_size("col"), lax.axis_size("depth")
    row, col, layer = lax.axis_index("row"), lax.axis_index("col"), lax.axis_index("depth")
    core, share = row % 2, (row // 2) * layers + layer
    blocks = order.shape[0]
    whole = blocks * TILE
    layouts = [(natural, NATURAL, jnp.arange(blocks))] + [(balanced, BALANCED, order)] * (STEPS - 1)
    layouts = layouts + [layouts[0]]

    def of_plane(packed):
        packed = packed.reshape(cols, 2, -1)
        both = lax.dynamic_index_in_dim(packed, col, 0, keepdims=False)
        return jnp.where(core == 0, both, both[::-1]).reshape(-1)

    def for_planes(packed):
        packed = packed.reshape(cols // 4, 4, 2, -1)
        packed = lax.dynamic_index_in_dim(packed, core, 2, keepdims=False)
        twice = jnp.concatenate([packed, packed], axis=1)
        return lax.dynamic_slice_in_dim(twice, col % 4, 4, 1).transpose(1, 0, 2).reshape(-1)

    part = None
    for step in range(STEPS):
        now, slots_in, columns = layouts[step]
        then, slots_out, _ = layouts[step + 1]
        if step > 0:
            own, other = in_plane(part)
        info = jnp.concatenate(
            [
                share[None],
                lax.dynamic_slice_in_dim(columns, 2 * col, 2, 0),
                branch[step][None],
                of_plane(now),
                for_planes(then),
            ]
        ).astype(jnp.int32)
        wide = 2 * TILE
        out = on_core(
            functools.partial(step_kernel, slots_in=slots_in, slots_out=slots_out, blocks=blocks),
            (cols * slots_out * LANES, TILE),
            scratch=(
                pltpu.VMEM((wide, whole), jnp.float32),
                pltpu.VMEM((wide, whole), jnp.bfloat16),
                pltpu.VMEM((wide, whole), jnp.bfloat16),
                pltpu.VMEM((wide, blocks * LANES), jnp.float32),
                pltpu.VMEM((blocks * LANES, whole), jnp.float32),
            ),
        )(info, own, other)
        part = sum_along_col(out.reshape(4, cols // 4, slots_out * LANES, TILE))

    strips = on_core(
        functools.partial(place_kernel, slots=NATURAL, blocks=blocks), (2 * LANES, whole)
    )(of_plane(natural), part, swap_cores(part))
    sharers, height = TILE // LANES, whole // rows
    cut = strips.reshape(2 * LANES, rows // 2, 2, height)
    cut = lax.dynamic_index_in_dim(cut, core, 2, keepdims=False).transpose(1, 0, 2)
    cut = jnp.broadcast_to(cut[:, None], (rows // 2, layers) + cut.shape[1:]).reshape(sharers, 2 * LANES, height)
    back = exchange(cut, ("row", "depth"), plane_groups())
    back = back.reshape(sharers, 2, LANES, height).transpose(1, 0, 2, 3).reshape(2 * TILE, height)
    return back.T


def local(density, pattern, branch):
    rows, cols, layers = lax.axis_size("row"), lax.axis_size("col"), lax.axis_size("depth")
    row, col, layer = lax.axis_index("row"), lax.axis_index("col"), lax.axis_index("depth")
    height, width = density.shape
    blocks = rows * pattern.shape[0]
    cut = density.T.reshape(2, rows // 2, layers, LANES, height)
    cut = lax.dynamic_index_in_dim(cut, layer, 2, keepdims=False).transpose(1, 0, 2, 3)
    cut = cut.reshape(rows // 2, 2 * LANES, height)
    marks = jnp.zeros((LANES, height), jnp.float32).at[:2, : pattern.shape[0]].set(pattern.T.astype(jnp.float32))
    cut = jnp.concatenate([cut, jnp.broadcast_to(marks[None], (rows // 2,) + marks.shape)], axis=1)
    cut = jnp.broadcast_to(cut[:, None], (rows // 2, 2) + cut.shape[1:]).reshape((rows,) + cut.shape[1:])
    got = exchange(cut, "row")
    strips = got[:, : 2 * LANES].transpose(1, 0, 2).reshape(2 * LANES, rows * height)
    marks = got[:, 2 * LANES : 2 * LANES + 2, : pattern.shape[0]].transpose(1, 0, 2).reshape(2, blocks)

    ids = jnp.arange(blocks)
    sent = jnp.zeros((LANES, TILE), jnp.float32).at[:2, :blocks].set(marks)
    seen = lax.all_gather(sent, "col")[:, :2, :blocks].reshape(blocks, blocks)
    columns = 2 * col + jnp.arange(2)
    held = jnp.where(columns[:, None] == ids, 1, marks.astype(jnp.int32))
    mine = slot_list(held, columns, NATURAL).reshape(2, NATURAL)
    part = on_core(functools.partial(pick_kernel, slots=NATURAL, blocks=blocks), (NATURAL * LANES, TILE))(
        lax.dynamic_index_in_dim(mine, row % 2, 0, keepdims=False), strips
    )
    own, other = in_plane(part)
    keep = jnp.where(ids[:, None] == ids[None, :], 1, seen.astype(jnp.int32))
    order = column_order(keep)
    moved = jnp.dot((order[:, None] == ids).astype(jnp.float32), keep.astype(jnp.float32)).astype(jnp.int32)

    def in_pairs(rows_of):
        return rows_of.reshape((cols, 2) + rows_of.shape[1:])

    natural = slot_list(in_pairs(keep), in_pairs(ids), NATURAL)
    balanced = slot_list(in_pairs(moved), in_pairs(order), BALANCED)
    spare = jnp.stack(
        [2 * NATURAL - in_pairs(keep).sum((1, 2)), 2 * BALANCED - in_pairs(moved).sum((1, 2))]
    )
    purified = sparse(own, other, natural, balanced, order, branch)
    return lax.cond(spare.min() >= 0, lambda: purified, lambda: dense(density, pattern, branch))


def solution(mesh):
    in_specs = (P("row", "col"), P("row", "col"), P())
    out_specs = P("row", "col")
    return jax.shard_map(local, mesh=mesh, in_specs=in_specs, out_specs=out_specs, check_vma=False)
```

profile of v0, /device:TPU:1, one launch (start us, length us, event | category | flops | bytes accessed | tf_op | source)
XLA Modules:
  0.0 361.2 jit_solution(16776278717594106787)
XLA Ops:
  2.8 10.2 %all-to-all-start.12 = ((f32[8,24,512]{2,1,0:T(8,128)}), f32[8,24,512]{2,1,0:T(8,128)S(1)}, u32[]{:S(2)}, u32[]{:S(2)}) async-start(f32[8,24,512]{2,1,0:T(8,128)} %bitcast.77), calls=%async_computation.12 | async-start | bytes 786432 | tf_op jit(solution)/shard_map/all_to_all | solution.py:18
  13.9 7.2 %all-to-all-done.12 = f32[8,24,512]{2,1,0:T(8,128)S(1)} async-done(((f32[8,24,512]{2,1,0:T(8,128)}), f32[8,24,512]{2,1,0:T(8,128)S(1)}, u32[]{:S(2)}, u32[]{:S(2)}) %all-to-all-start.12) | async-done | bytes 393248 | tf_op jit(solution)/shard_map/all_to_all | solution.py:18
  28.9 26.3 %all_gather.7 = f32[16,8,128]{2,1,0:T(8,128)S(1)} all-gather(f32[1,8,128]{2,1,0:T(8,128)S(1)} %scatter.9), channel_id=1, replica_groups=mesh['row'=8,'col'=16,'depth'=4] {'col'}, dimensions={0}, use_global_device_ids=true | all-gather | bytes 69632 | tf_op jit(solution)/shard_map/all_gather | solution.py:300
  58.0 9.3 %collective-permute-start.20 = (f32[16,144,128]{2,1,0:T(8,128)S(1)}, f32[16,144,128]{2,1,0:T(8,128)S(1)}, u32[]{:S(2)}, u32[]{:S(2)}) collective-permute-start(f32[16,144,128]{2,1,0:T(8,128)S(1)} %all-to-all-done.13.own_ref), channel_id=1, source_target_pairs={{0,64},{64,0},{128,192},{192,128},{256,320},{320,256},{384,448},{4... | collective-permute-start | bytes 3538952 | tf_op jit(solution)/shard_map/ppermute | solution.py:39
  69.7 6.3 %shard_map.40 = f32[1792,128]{1,0:T(8,128)S(1)} custom-call(s32[264]{0:T(512)S(1)} %concatenate.57.info_ref, f32[16,144,128]{2,1,0:T(8,128)S(1)} %all-to-all-done.13.own_ref, f32[16,144,128]{2,1,0:T(8,128)S(1)} %collective-permute-done.20.other_ref), custom_call_target="tpu_custom_call" | custom-call | tf_op jit(solution)/shard_map/pallas_call | solution.py:200
  84.5 5.5 %collective-permute-start.24 = (f32[2,112,128]{2,1,0:T(8,128)S(1)}, f32[2,112,128]{2,1,0:T(8,128)S(1)}, u32[]{:S(2)}, u32[]{:S(2)}) collective-permute-start(f32[2,112,128]{2,1,0:T(8,128)S(1)} %bitcast.277), channel_id=1, source_target_pairs={{0,56},{4,60},{8,0},{12,4},{16,8},{20,12},{24,16},{28,20},{32,24},... | collective-permute-start | bytes 344072 | tf_op jit(solution)/shard_map/ppermute | solution.py:27
  93.2 23.1 %all_to_all.106 = f32[4,112,128]{2,1,0:T(8,128)S(1)} all-to-all(f32[4,112,128]{2,1,0:T(8,128)S(1)} %maximum_add_fusion.1), channel_id=1, replica_groups={{0,16,32,48},{4,20,36,52},{8,24,40,56},{12,28,44,60},{1,17,33,49},{5,21..., dimensions={0} | all-to-all | bytes 458752 | tf_op jit(solution)/shard_map/all_to_all | solution.py:18
  116.4 18.9 %all_to_all.107.own_ref = f32[16,112,128]{2,1,0:T(8,128)S(1)} all-to-all(f32[16,112,128]{2,1,0:T(8,128)S(1)} %broadcast_in_dim.118), channel_id=1, replica_groups={{0,1,2,3,128,129,130,131,256,257,258,259,384,385,386,387},{64,65,66,67,..., dimensions={0} | all-to-all | bytes 1835008 | tf_op jit(solution)/shard_map/all_to_all | solution.py:18
  135.3 5.9 %collective-permute-start.25 = (f32[16,112,128]{2,1,0:T(8,128)S(1)}, f32[16,112,128]{2,1,0:T(8,128)S(1)}, u32[]{:S(2)}, u32[]{:S(2)}) collective-permute-start(f32[16,112,128]{2,1,0:T(8,128)S(1)} %all_to_all.107.own_ref), channel_id=1, source_target_pairs={{0,64},{64,0},{128,192},{192,128},{256,320},{320,256},{384,448},{4... | collective-permute-start | bytes 2752520 | tf_op jit(solution)/shard_map/ppermute | solution.py:39
  143.4 6.1 %shard_map.41 = f32[1792,128]{1,0:T(8,128)S(1)} custom-call(s32[256]{0:T(256)S(1)} %concatenate.56.info_ref, f32[16,112,128]{2,1,0:T(8,128)S(1)} %all_to_all.107.own_ref, f32[16,112,128]{2,1,0:T(8,128)S(1)} %collective-permute-done.25.other_ref), custom_call_target="tpu_custom_call" | custom-call | tf_op jit(solution)/shard_map/pallas_call | solution.py:200
  156.1 5.6 %collective-permute-start.28 = (f32[2,112,128]{2,1,0:T(8,128)S(1)}, f32[2,112,128]{2,1,0:T(8,128)S(1)}, u32[]{:S(2)}, u32[]{:S(2)}) collective-permute-start(f32[2,112,128]{2,1,0:T(8,128)S(1)} %bitcast.281), channel_id=1, source_target_pairs={{0,8},{4,12},{8,16},{12,20},{16,24},{20,28},{24,32},{28,36},{32,40... | collective-permute-start | bytes 344072 | tf_op jit(solution)/shard_map/ppermute | solution.py:27
  171.2 15.5 %all_to_all.108 = f32[4,112,128]{2,1,0:T(8,128)S(1)} all-to-all(f32[4,112,128]{2,1,0:T(8,128)S(1)} %maximum_add_fusion.2), channel_id=1, replica_groups={{0,16,32,48},{4,20,36,52},{8,24,40,56},{12,28,44,60},{1,17,33,49},{5,21..., dimensions={0} | all-to-all | bytes 458752 | tf_op jit(solution)/shard_map/all_to_all | solution.py:18
  186.8 14.0 %all_to_all.109.own_ref = f32[16,112,128]{2,1,0:T(8,128)S(1)} all-to-all(f32[16,112,128]{2,1,0:T(8,128)S(1)} %broadcast_in_dim.119), channel_id=1, replica_groups={{0,1,2,3,128,129,130,131,256,257,258,259,384,385,386,387},{64,65,66,67,..., dimensions={0} | all-to-all | bytes 1835008 | tf_op jit(solution)/shard_map/all_to_all | solution.py:18
  200.8 10.5 %collective-permute-start.30 = (f32[16,112,128]{2,1,0:T(8,128)S(1)}, f32[16,112,128]{2,1,0:T(8,128)S(1)}, u32[]{:S(2)}, u32[]{:S(2)}) collective-permute-start(f32[16,112,128]{2,1,0:T(8,128)S(1)} %all_to_all.109.own_ref), channel_id=1, source_target_pairs={{0,64},{64,0},{128,192},{192,128},{256,320},{320,256},{384,448},{4... | collective-permute-start | bytes 2752520 | tf_op jit(solution)/shard_map/ppermute | solution.py:39
  213.2 6.1 %shard_map.42 = f32[1792,128]{1,0:T(8,128)S(1)} custom-call(s32[256]{0:T(256)S(1)} %concatenate.55.info_ref, f32[16,112,128]{2,1,0:T(8,128)S(1)} %all_to_all.109.own_ref, f32[16,112,128]{2,1,0:T(8,128)S(1)} %collective-permute-done.30.other_ref), custom_call_target="tpu_custom_call" | custom-call | tf_op jit(solution)/shard_map/pallas_call | solution.py:200
  223.4 6.5 %collective-permute-start.32 = (f32[4,112,128]{2,1,0:T(8,128)S(1)}, f32[4,112,128]{2,1,0:T(8,128)S(1)}, u32[]{:S(2)}, u32[]{:S(2)}) collective-permute-start(f32[4,112,128]{2,1,0:T(8,128)S(1)} %bitcast.271), channel_id=1, source_target_pairs={{0,60},{4,0},{8,4},{12,8},{16,12},{20,16},{24,20},{28,24},{32,28},... | collective-permute-start | bytes 688136 | tf_op jit(solution)/shard_map/ppermute | solution.py:27
  231.9 5.5 %collective-permute-start.34 = (f32[2,112,128]{2,1,0:T(8,128)S(1)}, f32[2,112,128]{2,1,0:T(8,128)S(1)}, u32[]{:S(2)}, u32[]{:S(2)}) collective-permute-start(f32[2,112,128]{2,1,0:T(8,128)S(1)} %bitcast.279), channel_id=1, source_target_pairs={{0,56},{4,60},{8,0},{12,4},{16,8},{20,12},{24,16},{28,20},{32,24},... | collective-permute-start | bytes 344072 | tf_op jit(solution)/shard_map/ppermute | solution.py:27
  241.5 15.4 %all_to_all.110 = f32[4,112,128]{2,1,0:T(8,128)S(1)} all-to-all(f32[4,112,128]{2,1,0:T(8,128)S(1)} %maximum_add_fusion.3), channel_id=1, replica_groups={{0,16,32,48},{4,20,36,52},{8,24,40,56},{12,28,44,60},{1,17,33,49},{5,21..., dimensions={0} | all-to-all | bytes 458752 | tf_op jit(solution)/shard_map/all_to_all | solution.py:18
  257.0 14.0 %all_to_all.111.own_ref = f32[16,112,128]{2,1,0:T(8,128)S(1)} all-to-all(f32[16,112,128]{2,1,0:T(8,128)S(1)} %broadcast_in_dim.120), channel_id=1, replica_groups={{0,1,2,3,128,129,130,131,256,257,258,259,384,385,386,387},{64,65,66,67,..., dimensions={0} | all-to-all | bytes 1835008 | tf_op jit(solution)/shard_map/all_to_all | solution.py:18
  271.0 12.2 %collective-permute-start.35 = (f32[16,112,128]{2,1,0:T(8,128)S(1)}, f32[16,112,128]{2,1,0:T(8,128)S(1)}, u32[]{:S(2)}, u32[]{:S(2)}) collective-permute-start(f32[16,112,128]{2,1,0:T(8,128)S(1)} %all_to_all.111.own_ref), channel_id=1, source_target_pairs={{0,64},{64,0},{128,192},{192,128},{256,320},{320,256},{384,448},{4... | collective-permute-start | bytes 2752520 | tf_op jit(solution)/shard_map/ppermute | solution.py:39
  285.2 6.5 %shard_map.43 = f32[2304,128]{1,0:T(8,128)S(1)} custom-call(s32[320]{0:T(512)S(1)} %concatenate.53.info_ref, f32[16,112,128]{2,1,0:T(8,128)S(1)} %all_to_all.111.own_ref, f32[16,112,128]{2,1,0:T(8,128)S(1)} %collective-permute-done.35.other_ref), custom_call_target="tpu_custom_call" | custom-call | tf_op jit(solution)/shard_map/pallas_call | solution.py:200
  311.9 17.4 %all_to_all.112 = f32[4,144,128]{2,1,0:T(8,128)S(1)} all-to-all(f32[4,144,128]{2,1,0:T(8,128)S(1)} %maximum_add_fusion), channel_id=1, replica_groups={{0,16,32,48},{4,20,36,52},{8,24,40,56},{12,28,44,60},{1,17,33,49},{5,21..., dimensions={0} | all-to-all | bytes 589824 | tf_op jit(solution)/shard_map/all_to_all | solution.py:18
  329.3 11.9 %collective-permute-start.40 = (f32[144,128]{1,0:T(8,128)S(1)}, f32[144,128]{1,0:T(8,128)S(1)}, u32[]{:S(2)}, u32[]{:S(2)}) collective-permute-start(f32[144,128]{1,0:T(8,128)S(1)} %reduce_sum.164.own_ref), channel_id=1, source_target_pairs={{0,64},{64,0},{128,192},{192,128},{256,320},{320,256},{384,448},{4... | collective-permute-start | bytes 221192 | tf_op jit(solution)/shard_map/ppermute | solution.py:39
  350.1 8.2 %all-to-all-done.21 = f32[16,16,512]{2,1,0:T(8,128)S(1)} async-done(((f32[16,16,512]{2,1,0:T(8,128)}), f32[16,16,512]{2,1,0:T(8,128)S(1)}, u32[]{:S(2)}, u32[]{:S(2)}) %all-to-all-start.21) | async-done | bytes 524320 | tf_op jit(solution)/shard_map/all_to_all | solution.py:18
  (165 shorter events, 92.4 us)
Async XLA Ops:
  2.8 18.3 %all-to-all-start.12 = ((f32[8,24,512]{2,1,0:T(8,128)}), f32[8,24,512]{2,1,0:T(8,128)S(1)}, u32[]{:S(2)}, u32[]{:S(2)}) async-start(f32[8,24,512]{2,1,0:T(8,128)} %bitcast.77), calls=%async_computation.12 | async-start | bytes 786432 | tf_op jit(solution)/shard_map/all_to_all | solution.py:18
  25.0 33.0 %all-to-all-start.13 = ((f32[16,144,128]{2,1,0:T(8,128)}), f32[16,144,128]{2,1,0:T(8,128)S(1)}, u32[]{:S(2)}, u32[]{:S(2)}) async-start(f32[16,144,128]{2,1,0:T(8,128)} %broadcast_in_dim.117), calls=%async_computation.13 | async-start | bytes 2359296 | tf_op jit(solution)/shard_map/all_to_all | solution.py:18
  58.0 11.7 %collective-permute-start.20 = (f32[16,144,128]{2,1,0:T(8,128)S(1)}, f32[16,144,128]{2,1,0:T(8,128)S(1)}, u32[]{:S(2)}, u32[]{:S(2)}) collective-permute-start(f32[16,144,128]{2,1,0:T(8,128)S(1)} %all-to-all-done.13.own_ref), channel_id=1, source_target_pairs={{0,64},{64,0},{128,192},{192,128},{256,320},{320,256},{384,448},{4... | collective-permute-start | bytes 3538952 | tf_op jit(solution)/shard_map/ppermute | solution.py:39
  76.1 17.1 %collective-permute-start.21 = (f32[4,112,128]{2,1,0:T(8,128)S(1)}, f32[4,112,128]{2,1,0:T(8,128)S(1)}, u32[]{:S(2)}, u32[]{:S(2)}) collective-permute-start(f32[4,112,128]{2,1,0:T(8,128)S(1)} %bitcast.272), channel_id=1, source_target_pairs={{0,4},{4,8},{8,12},{12,16},{16,20},{20,24},{24,28},{28,32},{32,36}... | collective-permute-start | bytes 688136 | tf_op jit(solution)/shard_map/ppermute | solution.py:27
  78.0 15.1 %collective-permute-start.22 = (f32[4,112,128]{2,1,0:T(8,128)S(1)}, f32[4,112,128]{2,1,0:T(8,128)S(1)}, u32[]{:S(2)}, u32[]{:S(2)}) collective-permute-start(f32[4,112,128]{2,1,0:T(8,128)S(1)} %bitcast.269), channel_id=1, source_target_pairs={{0,60},{4,0},{8,4},{12,8},{16,12},{20,16},{24,20},{28,24},{32,28},... | collective-permute-start | bytes 688136 | tf_op jit(solution)/shard_map/ppermute | solution.py:27
  82.6 9.8 %collective-permute-start.23 = (f32[2,112,128]{2,1,0:T(8,128)S(1)}, f32[2,112,128]{2,1,0:T(8,128)S(1)}, u32[]{:S(2)}, u32[]{:S(2)}) collective-permute-start(f32[2,112,128]{2,1,0:T(8,128)S(1)} %bitcast.280), channel_id=1, source_target_pairs={{0,8},{4,12},{8,16},{12,20},{16,24},{20,28},{24,32},{28,36},{32,40... | collective-permute-start | bytes 344072 | tf_op jit(solution)/shard_map/ppermute | solution.py:27
  84.5 8.6 %collective-permute-start.24 = (f32[2,112,128]{2,1,0:T(8,128)S(1)}, f32[2,112,128]{2,1,0:T(8,128)S(1)}, u32[]{:S(2)}, u32[]{:S(2)}) collective-permute-start(f32[2,112,128]{2,1,0:T(8,128)S(1)} %bitcast.277), channel_id=1, source_target_pairs={{0,56},{4,60},{8,0},{12,4},{16,8},{20,12},{24,16},{28,20},{32,24},... | collective-permute-start | bytes 344072 | tf_op jit(solution)/shard_map/ppermute | solution.py:27
  135.3 8.0 %collective-permute-start.25 = (f32[16,112,128]{2,1,0:T(8,128)S(1)}, f32[16,112,128]{2,1,0:T(8,128)S(1)}, u32[]{:S(2)}, u32[]{:S(2)}) collective-permute-start(f32[16,112,128]{2,1,0:T(8,128)S(1)} %all_to_all.107.own_ref), channel_id=1, source_target_pairs={{0,64},{64,0},{128,192},{192,128},{256,320},{320,256},{384,448},{4... | collective-permute-start | bytes 2752520 | tf_op jit(solution)/shard_map/ppermute | solution.py:39
  149.6 21.6 %collective-permute-start.26 = (f32[4,112,128]{2,1,0:T(8,128)S(1)}, f32[4,112,128]{2,1,0:T(8,128)S(1)}, u32[]{:S(2)}, u32[]{:S(2)}) collective-permute-start(f32[4,112,128]{2,1,0:T(8,128)S(1)} %bitcast.273), channel_id=1, source_target_pairs={{0,4},{4,8},{8,12},{12,16},{16,20},{20,24},{24,28},{28,32},{32,36}... | collective-permute-start | bytes 688136 | tf_op jit(solution)/shard_map/ppermute | solution.py:27
  151.5 19.7 %collective-permute-start.27 = (f32[4,112,128]{2,1,0:T(8,128)S(1)}, f32[4,112,128]{2,1,0:T(8,128)S(1)}, u32[]{:S(2)}, u32[]{:S(2)}) collective-permute-start(f32[4,112,128]{2,1,0:T(8,128)S(1)} %bitcast.270), channel_id=1, source_target_pairs={{0,60},{4,0},{8,4},{12,8},{16,12},{20,16},{24,20},{28,24},{32,28},... | collective-permute-start | bytes 688136 | tf_op jit(solution)/shard_map/ppermute | solution.py:27
  156.1 10.9 %collective-permute-start.28 = (f32[2,112,128]{2,1,0:T(8,128)S(1)}, f32[2,112,128]{2,1,0:T(8,128)S(1)}, u32[]{:S(2)}, u32[]{:S(2)}) collective-permute-start(f32[2,112,128]{2,1,0:T(8,128)S(1)} %bitcast.281), channel_id=1, source_target_pairs={{0,8},{4,12},{8,16},{12,20},{16,24},{20,28},{24,32},{28,36},{32,40... | collective-permute-start | bytes 344072 | tf_op jit(solution)/shard_map/ppermute | solution.py:27
  161.7 9.4 %collective-permute-start.29 = (f32[2,112,128]{2,1,0:T(8,128)S(1)}, f32[2,112,128]{2,1,0:T(8,128)S(1)}, u32[]{:S(2)}, u32[]{:S(2)}) collective-permute-start(f32[2,112,128]{2,1,0:T(8,128)S(1)} %bitcast.278), channel_id=1, source_target_pairs={{0,56},{4,60},{8,0},{12,4},{16,8},{20,12},{24,16},{28,20},{32,24},... | collective-permute-start | bytes 344072 | tf_op jit(solution)/shard_map/ppermute | solution.py:27
  200.8 12.4 %collective-permute-start.30 = (f32[16,112,128]{2,1,0:T(8,128)S(1)}, f32[16,112,128]{2,1,0:T(8,128)S(1)}, u32[]{:S(2)}, u32[]{:S(2)}) collective-permute-start(f32[16,112,128]{2,1,0:T(8,128)S(1)} %all_to_all.109.own_ref), channel_id=1, source_target_pairs={{0,64},{64,0},{128,192},{192,128},{256,320},{320,256},{384,448},{4... | collective-permute-start | bytes 2752520 | tf_op jit(solution)/shard_map/ppermute | solution.py:39
  219.4 22.1 %collective-permute-start.31 = (f32[4,112,128]{2,1,0:T(8,128)S(1)}, f32[4,112,128]{2,1,0:T(8,128)S(1)}, u32[]{:S(2)}, u32[]{:S(2)}) collective-permute-start(f32[4,112,128]{2,1,0:T(8,128)S(1)} %bitcast.274), channel_id=1, source_target_pairs={{0,4},{4,8},{8,12},{12,16},{16,20},{20,24},{24,28},{28,32},{32,36}... | collective-permute-start | bytes 688136 | tf_op jit(solution)/shard_map/ppermute | solution.py:27
  223.4 18.0 %collective-permute-start.32 = (f32[4,112,128]{2,1,0:T(8,128)S(1)}, f32[4,112,128]{2,1,0:T(8,128)S(1)}, u32[]{:S(2)}, u32[]{:S(2)}) collective-permute-start(f32[4,112,128]{2,1,0:T(8,128)S(1)} %bitcast.271), channel_id=1, source_target_pairs={{0,60},{4,0},{8,4},{12,8},{16,12},{20,16},{24,20},{28,24},{32,28},... | collective-permute-start | bytes 688136 | tf_op jit(solution)/shard_map/ppermute | solution.py:27
  230.0 8.2 %collective-permute-start.33 = (f32[2,112,128]{2,1,0:T(8,128)S(1)}, f32[2,112,128]{2,1,0:T(8,128)S(1)}, u32[]{:S(2)}, u32[]{:S(2)}) collective-permute-start(f32[2,112,128]{2,1,0:T(8,128)S(1)} %bitcast.282), channel_id=1, source_target_pairs={{0,8},{4,12},{8,16},{12,20},{16,24},{20,28},{24,32},{28,36},{32,40... | collective-permute-start | bytes 344072 | tf_op jit(solution)/shard_map/ppermute | solution.py:27
  231.9 9.6 %collective-permute-start.34 = (f32[2,112,128]{2,1,0:T(8,128)S(1)}, f32[2,112,128]{2,1,0:T(8,128)S(1)}, u32[]{:S(2)}, u32[]{:S(2)}) collective-permute-start(f32[2,112,128]{2,1,0:T(8,128)S(1)} %bitcast.279), channel_id=1, source_target_pairs={{0,56},{4,60},{8,0},{12,4},{16,8},{20,12},{24,16},{28,20},{32,24},... | collective-permute-start | bytes 344072 | tf_op jit(solution)/shard_map/ppermute | solution.py:27
  271.0 14.3 %collective-permute-start.35 = (f32[16,112,128]{2,1,0:T(8,128)S(1)}, f32[16,112,128]{2,1,0:T(8,128)S(1)}, u32[]{:S(2)}, u32[]{:S(2)}) collective-permute-start(f32[16,112,128]{2,1,0:T(8,128)S(1)} %all_to_all.111.own_ref), channel_id=1, source_target_pairs={{0,64},{64,0},{128,192},{192,128},{256,320},{320,256},{384,448},{4... | collective-permute-start | bytes 2752520 | tf_op jit(solution)/shard_map/ppermute | solution.py:39
  291.8 20.0 %collective-permute-start.36 = (f32[4,144,128]{2,1,0:T(8,128)S(1)}, f32[4,144,128]{2,1,0:T(8,128)S(1)}, u32[]{:S(2)}, u32[]{:S(2)}) collective-permute-start(f32[4,144,128]{2,1,0:T(8,128)S(1)} %bitcast.268), channel_id=1, source_target_pairs={{0,4},{4,8},{8,12},{12,16},{16,20},{20,24},{24,28},{28,32},{32,36}... | collective-permute-start | bytes 884744 | tf_op jit(solution)/shard_map/ppermute | solution.py:27
  294.7 17.1 %collective-permute-start.37 = (f32[4,144,128]{2,1,0:T(8,128)S(1)}, f32[4,144,128]{2,1,0:T(8,128)S(1)}, u32[]{:S(2)}, u32[]{:S(2)}) collective-permute-start(f32[4,144,128]{2,1,0:T(8,128)S(1)} %bitcast.267), channel_id=1, source_target_pairs={{0,60},{4,0},{8,4},{12,8},{16,12},{20,16},{24,20},{28,24},{32,28},... | collective-permute-start | bytes 884744 | tf_op jit(solution)/shard_map/ppermute | solution.py:27
  298.3 10.1 %collective-permute-start.38 = (f32[2,144,128]{2,1,0:T(8,128)S(1)}, f32[2,144,128]{2,1,0:T(8,128)S(1)}, u32[]{:S(2)}, u32[]{:S(2)}) collective-permute-start(f32[2,144,128]{2,1,0:T(8,128)S(1)} %bitcast.276), channel_id=1, source_target_pairs={{0,8},{4,12},{8,16},{12,20},{16,24},{20,28},{24,32},{28,36},{32,40... | collective-permute-start | bytes 442376 | tf_op jit(solution)/shard_map/ppermute | solution.py:27
  300.3 11.5 %collective-permute-start.39 = (f32[2,144,128]{2,1,0:T(8,128)S(1)}, f32[2,144,128]{2,1,0:T(8,128)S(1)}, u32[]{:S(2)}, u32[]{:S(2)}) collective-permute-start(f32[2,144,128]{2,1,0:T(8,128)S(1)} %bitcast.275), channel_id=1, source_target_pairs={{0,56},{4,60},{8,0},{12,4},{16,8},{20,12},{24,16},{28,20},{32,24},... | collective-permute-start | bytes 442376 | tf_op jit(solution)/shard_map/ppermute | solution.py:27
  329.3 12.8 %collective-permute-start.40 = (f32[144,128]{1,0:T(8,128)S(1)}, f32[144,128]{1,0:T(8,128)S(1)}, u32[]{:S(2)}, u32[]{:S(2)}) collective-permute-start(f32[144,128]{1,0:T(8,128)S(1)} %reduce_sum.164.own_ref), channel_id=1, source_target_pairs={{0,64},{64,0},{128,192},{192,128},{256,320},{320,256},{384,448},{4... | collective-permute-start | bytes 221192 | tf_op jit(solution)/shard_map/ppermute | solution.py:39
  344.3 14.1 %all-to-all-start.21 = ((f32[16,16,512]{2,1,0:T(8,128)}), f32[16,16,512]{2,1,0:T(8,128)S(1)}, u32[]{:S(2)}, u32[]{:S(2)}) async-start(f32[16,16,512]{2,1,0:T(8,128)} %bitcast.114), calls=%async_computation.21 | async-start | bytes 1048576 | tf_op jit(solution)/shard_map/all_to_all | solution.py:18
  (4 other events, 42.6 us)
where the time goes:
time: 363 us; the launch traced here: 361 us
  blocking collectives  145 us (40%)
  starting transfers between devices  127 us (35%)
  waiting for transfers between devices  41.3 us (11%)
  Pallas kernels  26.5 us (7%)
  local copies, waits for them, and re-layouts  14.2 us (4%)
  other arithmetic  4.71 us (1%)
    all_to_all x7, blocking collectives, exchange(): lax.all_to_all(parts, axis, 0, 0, axis_index_groups=groups, tiled=True)  118 us
    ppermute x16, starting transfers between devices, shifted(): lax.ppermute(parts, 'col', [(z, (z + by) % cols) for z in range(cols)])  59.7 us
    ppermute x5, starting transfers between devices, swap_cores(): lax.ppermute(value, 'row', [(i, i ^ 1) for i in range(lax.axis_size('row'...  49.8 us
    pallas_call x6, Pallas kernels, call(): pl.pallas_call(kernel, out_shape=jax.ShapeDtypeStruct(shape, jnp.float32)...  26.5 us
    all_gather x1, blocking collectives, local(): seen = lax.all_gather(sent, 'col')[:, :2, :blocks].reshape(blocks, blocks)  26.3 us
    ppermute x16, waiting for transfers between devices, shifted(): lax.ppermute(parts, 'col', [(z, (z + by) % cols) for z in range(cols)])  20.8 us
    all_to_all x3, starting transfers between devices, exchange(): lax.all_to_all(parts, axis, 0, 0, axis_index_groups=groups, tiled=True)  17.6 us
    all_to_all x3, waiting for transfers between devices, exchange(): lax.all_to_all(parts, axis, 0, 0, axis_index_groups=groups, tiled=True)  15.4 us
  transfers between devices with their start and end apart: 24, of which 15 were waited for; matrix products, arithmetic and copies ran while one was open for 2% of the time, Pallas kernels for 0%

commit v1 on v0

--- a/solution.py
+++ b/solution.py
@@ -32,6 +32,22 @@
     far = [[c + 4 * m for m in range(cols // 4)] for c in range(4)]
     near = ahead[0] + shifted(ahead[1], 1) + shifted(ahead[3], -1)
     near = near + jnp.concatenate([shifted(ahead[2][:2], 2), shifted(ahead[2][2:], -2)])
+    return exchange(near, "col", far).sum(0)
+
+
+def sum_slots(own, one, two):
+    rows, cols, core = lax.axis_size("row"), lax.axis_size("col"), lax.axis_index("row") % 2
+    far = [[c + 4 * m for m in range(cols // 4)] for c in range(4)]
+
+    def apart(value, by):
+        steps = [(r, z, (z + by * (1 - 2 * (r % 2))) % cols) for r in range(rows) for z in range(cols)]
+        return lax.ppermute(value, ("row", "col"), [(r * cols + z, r * cols + to) for r, z, to in steps])
+
+    one, two = apart(one, 1), apart(two, 2)
+    half = lax.broadcasted_iota(jnp.int32, (one.shape[0], 1, 1, 1), 0) // two.shape[0]
+    got = one + jnp.where(half == core, jnp.concatenate([two, two]), 0.0)
+    theirs = swap_cores(lax.dynamic_index_in_dim(got, 1 - core, 1, keepdims=False))
+    near = own + lax.dynamic_index_in_dim(got, core, 1, keepdims=False) + theirs
     return exchange(near, "col", far).sum(0)
 
 
@@ -234,10 +250,15 @@
         return jnp.where(core == 0, both, both[::-1]).reshape(-1)
 
     def for_planes(packed):
-        packed = packed.reshape(cols // 4, 4, 2, -1)
-        packed = lax.dynamic_index_in_dim(packed, core, 2, keepdims=False)
-        twice = jnp.concatenate([packed, packed], axis=1)
-        return lax.dynamic_slice_in_dim(twice, col % 4, 4, 1).transpose(1, 0, 2).reshape(-1)
+        packed = packed.reshape(cols // 4, 4, -1)
+        slots = packed.shape[2] // 2
+
+        def of_class(by):
+            return lax.dynamic_index_in_dim(packed, (col + by) % 4, 1, keepdims=False)
+
+        own = lax.dynamic_slice_in_dim(of_class(0), core * slots, slots, 1)
+        two = lax.dynamic_slice_in_dim(of_class(2), core * (cols // 8), cols // 8, 0)
+        return jnp.concatenate([v.reshape(-1) for v in (own, of_class(1 + 2 * core), two)])
 
     part = None
     for step in range(STEPS):
@@ -266,7 +287,11 @@
                 pltpu.VMEM((blocks * LANES, whole), jnp.float32),
             ),
         )(info, own, other)
-        part = sum_along_col(out.reshape(4, cols // 4, slots_out * LANES, TILE))
+        quads, tall = cols // 4, slots_out * LANES
+        own, one, two = jnp.split(out, [quads * tall, 3 * quads * tall])
+        part = sum_slots(
+            own.reshape(quads, tall, TILE), one.reshape(quads, 2, tall, TILE), two.reshape(-1, 2, tall, TILE)
+        )
 
     strips = on_core(
         functools.partial(place_kernel, slots=NATURAL, blocks=blocks), (2 * LANES, whole)

time: 363 us -> 366 us (level)
  starting transfers between devices: 127 us -> 94.9 us
  waiting for transfers between devices: 41.3 us -> 67.3 us
  blocking collectives: 145 us -> 152 us
    ppermute x16 -> x8, starting transfers between devices: 59.7 us -> 30.3 us  [apart(): lax.ppermute(value, ('row', 'col'), [(r * cols + z, r * cols + to) for r,...]
    ppermute x16 -> x8, waiting for transfers between devices: 20.8 us -> 42.3 us  [apart(): lax.ppermute(value, ('row', 'col'), [(r * cols + z, r * cols + to) for r,...]
    all_to_all x7, blocking collectives: 118 us -> 126 us  [exchange(): lax.all_to_all(parts, axis, 0, 0, axis_index_groups=groups, tiled=True)]
    ppermute x5 -> x9, waiting for transfers between devices: 5.14 us -> 10.2 us  [swap_cores(): lax.ppermute(value, 'row', [(i, i ^ 1) for i in range(lax.axis_size('row'...]
    ppermute x5 -> x9, starting transfers between devices: 49.8 us -> 47 us  [swap_cores(): lax.ppermute(value, 'row', [(i, i ^ 1) for i in range(lax.axis_size('row'...]
  transfers between devices with their start and end apart: 24 -> 20, of which waited for: 15 -> 15; matrix products, arithmetic and copies ran while one was open for 2% -> 3% of each run, Pallas kernels for 0% -> 0%
where the time goes in v1:
time: 366 us; the launch traced here: 363 us
  blocking collectives  152 us (42%)
  starting transfers between devices  94.9 us (26%)
  waiting for transfers between devices  67.3 us (18%)
  Pallas kernels  26 us (7%)
  local copies, waits for them, and re-layouts  14.6 us (4%)
  other arithmetic  5.79 us (2%)
    all_to_all x7, blocking collectives, exchange(): lax.all_to_all(parts, axis, 0, 0, axis_index_groups=groups, tiled=True)  126 us
    ppermute x9, starting transfers between devices, swap_cores(): lax.ppermute(value, 'row', [(i, i ^ 1) for i in range(lax.axis_size('row'...  47 us
    ppermute x8, waiting for transfers between devices, apart(): lax.ppermute(value, ('row', 'col'), [(r * cols + z, r * cols + to) for r,...  42.3 us
    ppermute x8, starting transfers between devices, apart(): lax.ppermute(value, ('row', 'col'), [(r * cols + z, r * cols + to) for r,...  30.3 us
    all_gather x1, blocking collectives, local(): seen = lax.all_gather(sent, 'col')[:, :2, :blocks].reshape(blocks, blocks)  26.3 us
    pallas_call x6, Pallas kernels, call(): pl.pallas_call(kernel, out_shape=jax.ShapeDtypeStruct(shape, jnp.float32)...  26 us
    all_to_all x3, starting transfers between devices, exchange(): lax.all_to_all(parts, axis, 0, 0, axis_index_groups=groups, tiled=True)  17.6 us
    all_to_all x3, waiting for transfers between devices, exchange(): lax.all_to_all(parts, axis, 0, 0, axis_index_groups=groups, tiled=True)  14.8 us
  transfers between devices with their start and end apart: 20, of which 15 were waited for; matrix products, arithmetic and copies ran while one was open for 3% of the time, Pallas kernels for 0%

profile of v1, /device:TPU:1, one launch (start us, length us, event | category | flops | bytes accessed | tf_op | source)
XLA Modules:
  0.0 363.4 jit_solution(17903398218236810131)
XLA Ops:
  2.8 10.2 %all-to-all-start.12 = ((f32[8,24,512]{2,1,0:T(8,128)}), f32[8,24,512]{2,1,0:T(8,128)S(1)}, u32[]{:S(2)}, u32[]{:S(2)}) async-start(f32[8,24,512]{2,1,0:T(8,128)} %bitcast.77), calls=%async_computation.12 | async-start | bytes 786432 | tf_op jit(solution)/shard_map/all_to_all | solution.py:18
  13.9 7.2 %all-to-all-done.12 = f32[8,24,512]{2,1,0:T(8,128)S(1)} async-done(((f32[8,24,512]{2,1,0:T(8,128)}), f32[8,24,512]{2,1,0:T(8,128)S(1)}, u32[]{:S(2)}, u32[]{:S(2)}) %all-to-all-start.12) | async-done | bytes 393248 | tf_op jit(solution)/shard_map/all_to_all | solution.py:18
  28.9 26.3 %all_gather.7 = f32[16,8,128]{2,1,0:T(8,128)S(1)} all-gather(f32[1,8,128]{2,1,0:T(8,128)S(1)} %scatter.9), channel_id=1, replica_groups=mesh['row'=8,'col'=16,'depth'=4] {'col'}, dimensions={0}, use_global_device_ids=true | all-gather | bytes 69632 | tf_op jit(solution)/shard_map/all_gather | solution.py:325
  58.1 9.3 %collective-permute-start.20 = (f32[16,144,128]{2,1,0:T(8,128)S(1)}, f32[16,144,128]{2,1,0:T(8,128)S(1)}, u32[]{:S(2)}, u32[]{:S(2)}) collective-permute-start(f32[16,144,128]{2,1,0:T(8,128)S(1)} %all-to-all-done.13.own_ref), channel_id=1, source_target_pairs={{0,64},{64,0},{128,192},{192,128},{256,320},{320,256},{384,448},{4... | collective-permute-start | bytes 3538952 | tf_op jit(solution)/shard_map/ppermute | solution.py:55
  69.9 6.1 %shard_map.40 = f32[1792,128]{1,0:T(8,128)S(1)} custom-call(s32[264]{0:T(512)S(1)} %concatenate.47.info_ref, f32[16,144,128]{2,1,0:T(8,128)S(1)} %all-to-all-done.13.own_ref, f32[16,144,128]{2,1,0:T(8,128)S(1)} %collective-permute-done.20.other_ref), custom_call_target="tpu_custom_call" | custom-call | tf_op jit(solution)/shard_map/pallas_call | solution.py:216
  81.8 8.0 %collective-permute-done.22 = f32[2,2,112,128]{3,2,1,0:T(8,128)S(1)} collective-permute-done((f32[2,2,112,128]{3,2,1,0:T(8,128)S(1)}, f32[2,2,112,128]{3,2,1,0:T(8,128)S(1)}, u32[]{:S(2)}, u32[]{:S(2)}) %collective-permute-start.22) | collective-permute-done | bytes 229408 | tf_op jit(solution)/shard_map/ppermute | solution.py:44
  93.6 22.7 %all_to_all.106 = f32[4,112,128]{2,1,0:T(8,128)S(1)} all-to-all(f32[4,112,128]{2,1,0:T(8,128)S(1)} %fusion.57), channel_id=1, replica_groups={{0,16,32,48},{4,20,36,52},{8,24,40,56},{12,28,44,60},{1,17,33,49},{5,21..., dimensions={0} | all-to-all | bytes 458752 | tf_op jit(solution)/shard_map/all_to_all | solution.py:18
  116.4 18.0 %all_to_all.107.own_ref = f32[16,112,128]{2,1,0:T(8,128)S(1)} all-to-all(f32[16,112,128]{2,1,0:T(8,128)S(1)} %broadcast_in_dim.152), channel_id=1, replica_groups={{0,1,2,3,128,129,130,131,256,257,258,259,384,385,386,387},{64,65,66,67,..., dimensions={0} | all-to-all | bytes 1835008 | tf_op jit(solution)/shard_map/all_to_all | solution.py:18
  134.4 7.1 %collective-permute-start.24 = (f32[16,112,128]{2,1,0:T(8,128)S(1)}, f32[16,112,128]{2,1,0:T(8,128)S(1)}, u32[]{:S(2)}, u32[]{:S(2)}) collective-permute-start(f32[16,112,128]{2,1,0:T(8,128)S(1)} %all_to_all.107.own_ref), channel_id=1, source_target_pairs={{0,64},{64,0},{128,192},{192,128},{256,320},{320,256},{384,448},{4... | collective-permute-start | bytes 2752520 | tf_op jit(solution)/shard_map/ppermute | solution.py:55
  143.5 6.0 %shard_map.41 = f32[1792,128]{1,0:T(8,128)S(1)} custom-call(s32[256]{0:T(256)S(1)} %concatenate.46.info_ref, f32[16,112,128]{2,1,0:T(8,128)S(1)} %all_to_all.107.own_ref, f32[16,112,128]{2,1,0:T(8,128)S(1)} %collective-permute-done.24.other_ref), custom_call_target="tpu_custom_call" | custom-call | tf_op jit(solution)/shard_map/pallas_call | solution.py:216
  157.4 11.4 %collective-permute-done.26 = f32[2,2,112,128]{3,2,1,0:T(8,128)S(1)} collective-permute-done((f32[2,2,112,128]{3,2,1,0:T(8,128)S(1)}, f32[2,2,112,128]{3,2,1,0:T(8,128)S(1)}, u32[]{:S(2)}, u32[]{:S(2)}) %collective-permute-start.26) | collective-permute-done | bytes 229408 | tf_op jit(solution)/shard_map/ppermute | solution.py:44
  172.3 17.5 %all_to_all.108 = f32[4,112,128]{2,1,0:T(8,128)S(1)} all-to-all(f32[4,112,128]{2,1,0:T(8,128)S(1)} %fusion.56), channel_id=1, replica_groups={{0,16,32,48},{4,20,36,52},{8,24,40,56},{12,28,44,60},{1,17,33,49},{5,21..., dimensions={0} | all-to-all | bytes 458752 | tf_op jit(solution)/shard_map/all_to_all | solution.py:18
  190.0 17.1 %all_to_all.109.own_ref = f32[16,112,128]{2,1,0:T(8,128)S(1)} all-to-all(f32[16,112,128]{2,1,0:T(8,128)S(1)} %broadcast_in_dim.153), channel_id=1, replica_groups={{0,1,2,3,128,129,130,131,256,257,258,259,384,385,386,387},{64,65,66,67,..., dimensions={0} | all-to-all | bytes 1835008 | tf_op jit(solution)/shard_map/all_to_all | solution.py:18
  213.7 6.0 %shard_map.42 = f32[1792,128]{1,0:T(8,128)S(1)} custom-call(s32[256]{0:T(256)S(1)} %concatenate.45.info_ref, f32[16,112,128]{2,1,0:T(8,128)S(1)} %all_to_all.109.own_ref, f32[16,112,128]{2,1,0:T(8,128)S(1)} %collective-permute-done.28.other_ref), custom_call_target="tpu_custom_call" | custom-call | tf_op jit(solution)/shard_map/pallas_call | solution.py:216
  221.7 6.7 %collective-permute-start.30 = (f32[2,2,112,128]{3,2,1,0:T(8,128)S(1)}, f32[2,2,112,128]{3,2,1,0:T(8,128)S(1)}, u32[]{:S(2)}, u32[]{:S(2)}) collective-permute-start(f32[2,2,112,128]{3,2,1,0:T(8,128)S(1)} %bitcast.286), channel_id=1, source_target_pairs={{0,8},{4,12},{8,16},{12,20},{16,24},{20,28},{24,32},{28,36},{32,40... | collective-permute-start | bytes 688136 | tf_op jit(solution)/shard_map/ppermute | solution.py:44
  228.4 11.6 %collective-permute-done.30 = f32[2,2,112,128]{3,2,1,0:T(8,128)S(1)} collective-permute-done((f32[2,2,112,128]{3,2,1,0:T(8,128)S(1)}, f32[2,2,112,128]{3,2,1,0:T(8,128)S(1)}, u32[]{:S(2)}, u32[]{:S(2)}) %collective-permute-start.30) | collective-permute-done | bytes 229408 | tf_op jit(solution)/shard_map/ppermute | solution.py:44
  244.2 17.5 %all_to_all.110 = f32[4,112,128]{2,1,0:T(8,128)S(1)} all-to-all(f32[4,112,128]{2,1,0:T(8,128)S(1)} %fusion.55), channel_id=1, replica_groups={{0,16,32,48},{4,20,36,52},{8,24,40,56},{12,28,44,60},{1,17,33,49},{5,21..., dimensions={0} | all-to-all | bytes 458752 | tf_op jit(solution)/shard_map/all_to_all | solution.py:18
  261.8 14.1 %all_to_all.111.own_ref = f32[16,112,128]{2,1,0:T(8,128)S(1)} all-to-all(f32[16,112,128]{2,1,0:T(8,128)S(1)} %broadcast_in_dim.154), channel_id=1, replica_groups={{0,1,2,3,128,129,130,131,256,257,258,259,384,385,386,387},{64,65,66,67,..., dimensions={0} | all-to-all | bytes 1835008 | tf_op jit(solution)/shard_map/all_to_all | solution.py:18
  275.9 7.5 %collective-permute-start.32 = (f32[16,112,128]{2,1,0:T(8,128)S(1)}, f32[16,112,128]{2,1,0:T(8,128)S(1)}, u32[]{:S(2)}, u32[]{:S(2)}) collective-permute-start(f32[16,112,128]{2,1,0:T(8,128)S(1)} %all_to_all.111.own_ref), channel_id=1, source_target_pairs={{0,64},{64,0},{128,192},{192,128},{256,320},{320,256},{384,448},{4... | collective-permute-start | bytes 2752520 | tf_op jit(solution)/shard_map/ppermute | solution.py:55
  285.5 6.4 %shard_map.43 = f32[2304,128]{1,0:T(8,128)S(1)} custom-call(s32[320]{0:T(512)S(1)} %concatenate.44.info_ref, f32[16,112,128]{2,1,0:T(8,128)S(1)} %all_to_all.111.own_ref, f32[16,112,128]{2,1,0:T(8,128)S(1)} %collective-permute-done.32.other_ref), custom_call_target="tpu_custom_call" | custom-call | tf_op jit(solution)/shard_map/pallas_call | solution.py:216
  300.1 11.3 %collective-permute-done.34 = f32[2,2,144,128]{3,2,1,0:T(8,128)S(1)} collective-permute-done((f32[2,2,144,128]{3,2,1,0:T(8,128)S(1)}, f32[2,2,144,128]{3,2,1,0:T(8,128)S(1)}, u32[]{:S(2)}, u32[]{:S(2)}) %collective-permute-start.34) | collective-permute-done | bytes 294944 | tf_op jit(solution)/shard_map/ppermute | solution.py:44
  315.1 18.9 %all_to_all.112 = f32[4,144,128]{2,1,0:T(8,128)S(1)} all-to-all(f32[4,144,128]{2,1,0:T(8,128)S(1)} %fusion.54), channel_id=1, replica_groups={{0,16,32,48},{4,20,36,52},{8,24,40,56},{12,28,44,60},{1,17,33,49},{5,21..., dimensions={0} | all-to-all | bytes 589824 | tf_op jit(solution)/shard_map/all_to_all | solution.py:18
  334.0 9.3 %collective-permute-start.36 = (f32[144,128]{1,0:T(8,128)S(1)}, f32[144,128]{1,0:T(8,128)S(1)}, u32[]{:S(2)}, u32[]{:S(2)}) collective-permute-start(f32[144,128]{1,0:T(8,128)S(1)} %reduce_sum.164.own_ref), channel_id=1, source_target_pairs={{0,64},{64,0},{128,192},{192,128},{256,320},{320,256},{384,448},{4... | collective-permute-start | bytes 221192 | tf_op jit(solution)/shard_map/ppermute | solution.py:55
  352.9 7.6 %all-to-all-done.21 = f32[16,16,512]{2,1,0:T(8,128)S(1)} async-done(((f32[16,16,512]{2,1,0:T(8,128)}), f32[16,16,512]{2,1,0:T(8,128)S(1)}, u32[]{:S(2)}, u32[]{:S(2)}) %all-to-all-start.21) | async-done | bytes 524320 | tf_op jit(solution)/shard_map/all_to_all | solution.py:18
  (169 shorter events, 79.0 us)
Async XLA Ops:
  1.2 12.0 %copy-start.2 = (s32[4]{0:T(128)S(1)}, s32[4]{0:T(128)}, u32[]{:S(2)}) copy-start(s32[4]{0:T(128)} %param.11) | copy-start | bytes 52
  2.8 18.3 %all-to-all-start.12 = ((f32[8,24,512]{2,1,0:T(8,128)}), f32[8,24,512]{2,1,0:T(8,128)S(1)}, u32[]{:S(2)}, u32[]{:S(2)}) async-start(f32[8,24,512]{2,1,0:T(8,128)} %bitcast.77), calls=%async_computation.12 | async-start | bytes 786432 | tf_op jit(solution)/shard_map/all_to_all | solution.py:18
  25.0 33.1 %all-to-all-start.13 = ((f32[16,144,128]{2,1,0:T(8,128)}), f32[16,144,128]{2,1,0:T(8,128)S(1)}, u32[]{:S(2)}, u32[]{:S(2)}) async-start(f32[16,144,128]{2,1,0:T(8,128)} %broadcast_in_dim.149), calls=%async_computation.13 | async-start | bytes 2359296 | tf_op jit(solution)/shard_map/all_to_all | solution.py:18
  58.1 11.7 %collective-permute-start.20 = (f32[16,144,128]{2,1,0:T(8,128)S(1)}, f32[16,144,128]{2,1,0:T(8,128)S(1)}, u32[]{:S(2)}, u32[]{:S(2)}) collective-permute-start(f32[16,144,128]{2,1,0:T(8,128)S(1)} %all-to-all-done.13.own_ref), channel_id=1, source_target_pairs={{0,64},{64,0},{128,192},{192,128},{256,320},{320,256},{384,448},{4... | collective-permute-start | bytes 3538952 | tf_op jit(solution)/shard_map/ppermute | solution.py:55
  76.0 13.8 %collective-permute-start.21 = (f32[4,2,112,128]{3,2,1,0:T(8,128)S(1)}, f32[4,2,112,128]{3,2,1,0:T(8,128)S(1)}, u32[]{:S(2)}, u32[]{:S(2)}) collective-permute-start(f32[4,2,112,128]{3,2,1,0:T(8,128)S(1)} %bitcast.280), channel_id=1, source_target_pairs={{0,4},{4,8},{8,12},{12,16},{16,20},{20,24},{24,28},{28,32},{32,36}... | collective-permute-start | bytes 1376264 | tf_op jit(solution)/shard_map/ppermute | solution.py:44
  78.0 11.8 %collective-permute-start.22 = (f32[2,2,112,128]{3,2,1,0:T(8,128)S(1)}, f32[2,2,112,128]{3,2,1,0:T(8,128)S(1)}, u32[]{:S(2)}, u32[]{:S(2)}) collective-permute-start(f32[2,2,112,128]{3,2,1,0:T(8,128)S(1)} %bitcast.284), channel_id=1, source_target_pairs={{0,8},{4,12},{8,16},{12,20},{16,24},{20,28},{24,32},{28,36},{32,40... | collective-permute-start | bytes 688136 | tf_op jit(solution)/shard_map/ppermute | solution.py:44
  90.0 3.6 collective-permute-start.23
  134.4 9.1 %collective-permute-start.24 = (f32[16,112,128]{2,1,0:T(8,128)S(1)}, f32[16,112,128]{2,1,0:T(8,128)S(1)}, u32[]{:S(2)}, u32[]{:S(2)}) collective-permute-start(f32[16,112,128]{2,1,0:T(8,128)S(1)} %all_to_all.107.own_ref), channel_id=1, source_target_pairs={{0,64},{64,0},{128,192},{192,128},{256,320},{320,256},{384,448},{4... | collective-permute-start | bytes 2752520 | tf_op jit(solution)/shard_map/ppermute | solution.py:55
  149.6 19.2 %collective-permute-start.25 = (f32[4,2,112,128]{3,2,1,0:T(8,128)S(1)}, f32[4,2,112,128]{3,2,1,0:T(8,128)S(1)}, u32[]{:S(2)}, u32[]{:S(2)}) collective-permute-start(f32[4,2,112,128]{3,2,1,0:T(8,128)S(1)} %bitcast.281), channel_id=1, source_target_pairs={{0,4},{4,8},{8,12},{12,16},{16,20},{20,24},{24,28},{28,32},{32,36}... | collective-permute-start | bytes 1376264 | tf_op jit(solution)/shard_map/ppermute | solution.py:44
  151.5 17.2 %collective-permute-start.26 = (f32[2,2,112,128]{3,2,1,0:T(8,128)S(1)}, f32[2,2,112,128]{3,2,1,0:T(8,128)S(1)}, u32[]{:S(2)}, u32[]{:S(2)}) collective-permute-start(f32[2,2,112,128]{3,2,1,0:T(8,128)S(1)} %bitcast.285), channel_id=1, source_target_pairs={{0,8},{4,12},{8,16},{12,20},{16,24},{20,28},{24,32},{28,36},{32,40... | collective-permute-start | bytes 688136 | tf_op jit(solution)/shard_map/ppermute | solution.py:44
  168.9 3.4 collective-permute-start.27
  207.1 6.6 %collective-permute-start.28 = (f32[16,112,128]{2,1,0:T(8,128)S(1)}, f32[16,112,128]{2,1,0:T(8,128)S(1)}, u32[]{:S(2)}, u32[]{:S(2)}) collective-permute-start(f32[16,112,128]{2,1,0:T(8,128)S(1)} %all_to_all.109.own_ref), channel_id=1, source_target_pairs={{0,64},{64,0},{128,192},{192,128},{256,320},{320,256},{384,448},{4... | collective-permute-start | bytes 2752520 | tf_op jit(solution)/shard_map/ppermute | solution.py:55
  219.7 20.3 %collective-permute-start.29 = (f32[4,2,112,128]{3,2,1,0:T(8,128)S(1)}, f32[4,2,112,128]{3,2,1,0:T(8,128)S(1)}, u32[]{:S(2)}, u32[]{:S(2)}) collective-permute-start(f32[4,2,112,128]{3,2,1,0:T(8,128)S(1)} %bitcast.282), channel_id=1, source_target_pairs={{0,4},{4,8},{8,12},{12,16},{16,20},{20,24},{24,28},{28,32},{32,36}... | collective-permute-start | bytes 1376264 | tf_op jit(solution)/shard_map/ppermute | solution.py:44
  221.7 18.4 %collective-permute-start.30 = (f32[2,2,112,128]{3,2,1,0:T(8,128)S(1)}, f32[2,2,112,128]{3,2,1,0:T(8,128)S(1)}, u32[]{:S(2)}, u32[]{:S(2)}) collective-permute-start(f32[2,2,112,128]{3,2,1,0:T(8,128)S(1)} %bitcast.286), channel_id=1, source_target_pairs={{0,8},{4,12},{8,16},{12,20},{16,24},{20,28},{24,32},{28,36},{32,40... | collective-permute-start | bytes 688136 | tf_op jit(solution)/shard_map/ppermute | solution.py:44
  240.2 4.0 %collective-permute-start.31 = (f32[4,112,128]{2,1,0:T(8,128)S(1)}, f32[4,112,128]{2,1,0:T(8,128)S(1)}, u32[]{:S(2)}, u32[]{:S(2)}) collective-permute-start(f32[4,112,128]{2,1,0:T(8,128)S(1)} %dynamic-slice_bitcast_fusion.5), channel_id=1, source_target_pairs={{0,64},{64,0},{128,192},{192,128},{256,320},{320,256},{384,448},{4... | collective-permute-start | bytes 688136 | tf_op jit(solution)/shard_map/ppermute | solution.py:55
  275.9 9.5 %collective-permute-start.32 = (f32[16,112,128]{2,1,0:T(8,128)S(1)}, f32[16,112,128]{2,1,0:T(8,128)S(1)}, u32[]{:S(2)}, u32[]{:S(2)}) collective-permute-start(f32[16,112,128]{2,1,0:T(8,128)S(1)} %all_to_all.111.own_ref), channel_id=1, source_target_pairs={{0,64},{64,0},{128,192},{192,128},{256,320},{320,256},{384,448},{4... | collective-permute-start | bytes 2752520 | tf_op jit(solution)/shard_map/ppermute | solution.py:55
  291.9 19.5 %collective-permute-start.33 = (f32[4,2,144,128]{3,2,1,0:T(8,128)S(1)}, f32[4,2,144,128]{3,2,1,0:T(8,128)S(1)}, u32[]{:S(2)}, u32[]{:S(2)}) collective-permute-start(f32[4,2,144,128]{3,2,1,0:T(8,128)S(1)} %bitcast.277), channel_id=1, source_target_pairs={{0,4},{4,8},{8,12},{12,16},{16,20},{20,24},{24,28},{28,32},{32,36}... | collective-permute-start | bytes 1769480 | tf_op jit(solution)/shard_map/ppermute | solution.py:44
  294.5 16.9 %collective-permute-start.34 = (f32[2,2,144,128]{3,2,1,0:T(8,128)S(1)}, f32[2,2,144,128]{3,2,1,0:T(8,128)S(1)}, u32[]{:S(2)}, u32[]{:S(2)}) collective-permute-start(f32[2,2,144,128]{3,2,1,0:T(8,128)S(1)} %bitcast.283), channel_id=1, source_target_pairs={{0,8},{4,12},{8,16},{12,20},{16,24},{20,28},{24,32},{28,36},{32,40... | collective-permute-start | bytes 884744 | tf_op jit(solution)/shard_map/ppermute | solution.py:44
  311.6 3.5 collective-permute-start.35
  334.0 10.2 %collective-permute-start.36 = (f32[144,128]{1,0:T(8,128)S(1)}, f32[144,128]{1,0:T(8,128)S(1)}, u32[]{:S(2)}, u32[]{:S(2)}) collective-permute-start(f32[144,128]{1,0:T(8,128)S(1)} %reduce_sum.164.own_ref), channel_id=1, source_target_pairs={{0,64},{64,0},{128,192},{192,128},{256,320},{320,256},{384,448},{4... | collective-permute-start | bytes 221192 | tf_op jit(solution)/shard_map/ppermute | solution.py:55
  346.4 15.0 %copy-start = (f32[512,256]{1,0:T(8,128)S(1)}, f32[512,256]{1,0:T(8,128)}, u32[]{:S(2)}) copy-start(f32[512,256]{1,0:T(8,128)} %param.9) | copy-start | bytes 1572868
  346.4 15.0 %copy-start.3 = (s32[4,2]{0,1:T(2,128)S(1)}, s32[4,2]{0,1:T(2,128)}, u32[]{:S(2)}) copy-start(s32[4,2]{0,1:T(2,128)} %param.10) | copy-start | bytes 100
  346.4 14.1 %all-to-all-start.21 = ((f32[16,16,512]{2,1,0:T(8,128)}), f32[16,16,512]{2,1,0:T(8,128)S(1)}, u32[]{:S(2)}, u32[]{:S(2)}) async-start(f32[16,16,512]{2,1,0:T(8,128)} %bitcast.112), calls=%async_computation.21 | async-start | bytes 1048576 | tf_op jit(solution)/shard_map/all_to_all | solution.py:18
  362.6 0.8 copy-start.1

commit v2 on v0

--- a/solution.py
+++ b/solution.py
@@ -297,14 +297,21 @@
 
     ids = jnp.arange(blocks)
     sent = jnp.zeros((LANES, TILE), jnp.float32).at[:2, :blocks].set(marks)
-    seen = lax.all_gather(sent, "col")[:, :2, :blocks].reshape(blocks, blocks)
+    steps = [(r, z, y, (z - r // 2 * layers - y) % cols) for r in range(rows) for z in range(cols) for y in range(layers)]
+    ahead = lax.ppermute(
+        sent,
+        ("row", "col", "depth"),
+        [((r * cols + z) * layers + y, (r * cols + to) * layers + y) for r, z, y, to in steps],
+    )
     columns = 2 * col + jnp.arange(2)
     held = jnp.where(columns[:, None] == ids, 1, marks.astype(jnp.int32))
     mine = slot_list(held, columns, NATURAL).reshape(2, NATURAL)
     part = on_core(functools.partial(pick_kernel, slots=NATURAL, blocks=blocks), (NATURAL * LANES, TILE))(
         lax.dynamic_index_in_dim(mine, row % 2, 0, keepdims=False), strips
     )
-    own, other = in_plane(part)
+    own, other = in_plane(jnp.concatenate([part, ahead]))
+    seen = own[:, NATURAL * LANES : NATURAL * LANES + 2, :blocks].reshape(2 * cols, blocks)
+    seen = lax.dynamic_slice_in_dim(jnp.concatenate([seen, seen]), 2 * (cols - col), 2 * cols, 0)
     keep = jnp.where(ids[:, None] == ids[None, :], 1, seen.astype(jnp.int32))
     order = column_order(keep)
     moved = jnp.dot((order[:, None] == ids).astype(jnp.float32), keep.astype(jnp.float32)).astype(jnp.int32)

time: 363 us -> 361 us (level)
  blocking collectives: 145 us -> 125 us
  waiting for transfers between devices: 41.3 us -> 56.9 us
    all_gather x1 -> x0, blocking collectives: 26.3 us -> none  [local(): seen = lax.all_gather(sent, 'col')[:, :2, :blocks].reshape(blocks, blocks)]
    all_to_all x3, waiting for transfers between devices: 15.4 us -> 31.5 us  [exchange(): lax.all_to_all(parts, axis, 0, 0, axis_index_groups=groups, tiled=True)]
    ppermute x5, starting transfers between devices: 49.8 us -> 34.5 us  [swap_cores(): lax.ppermute(value, 'row', [(i, i ^ 1) for i in range(lax.axis_size('row'...]
    all_to_all x3, starting transfers between devices: 17.6 us -> 28 us  [exchange(): lax.all_to_all(parts, axis, 0, 0, axis_index_groups=groups, tiled=True)]
    all_to_all x7, blocking collectives: 118 us -> 125 us  [exchange(): lax.all_to_all(parts, axis, 0, 0, axis_index_groups=groups, tiled=True)]
  transfers between devices with their start and end apart: 24 -> 25, of which waited for: 15 -> 16; matrix products, arithmetic and copies ran while one was open for 2% -> 2% of each run, Pallas kernels for 0% -> 0%
where the time goes in v2:
time: 361 us; the launch traced here: 356 us
  starting transfers between devices  126 us (35%)
  blocking collectives  125 us (35%)
  waiting for transfers between devices  56.9 us (16%)
  Pallas kernels  26.4 us (7%)
  local copies, waits for them, and re-layouts  14.1 us (4%)
  other arithmetic  5.5 us (2%)
    all_to_all x7, blocking collectives, exchange(): lax.all_to_all(parts, axis, 0, 0, axis_index_groups=groups, tiled=True)  125 us
    ppermute x16, starting transfers between devices, shifted(): lax.ppermute(parts, 'col', [(z, (z + by) % cols) for z in range(cols)])  62.4 us
    ppermute x5, starting transfers between devices, swap_cores(): lax.ppermute(value, 'row', [(i, i ^ 1) for i in range(lax.axis_size('row'...  34.5 us
    all_to_all x3, waiting for transfers between devices, exchange(): lax.all_to_all(parts, axis, 0, 0, axis_index_groups=groups, tiled=True)  31.5 us
    all_to_all x3, starting transfers between devices, exchange(): lax.all_to_all(parts, axis, 0, 0, axis_index_groups=groups, tiled=True)  28 us
    pallas_call x6, Pallas kernels, call(): pl.pallas_call(kernel, out_shape=jax.ShapeDtypeStruct(shape, jnp.float32)...  26.4 us
    ppermute x16, waiting for transfers between devices, shifted(): lax.ppermute(parts, 'col', [(z, (z + by) % cols) for z in range(cols)])  20.5 us
  transfers between devices with their start and end apart: 25, of which 16 were waited for; matrix products, arithmetic and copies ran while one was open for 2% of the time, Pallas kernels for 0%

profile of v2, /device:TPU:1, one launch (start us, length us, event | category | flops | bytes accessed | tf_op | source)
XLA Modules:
  0.0 356.1 jit_solution(14798832269639126532)
XLA Ops:
  2.8 10.2 %all-to-all-start.12 = ((f32[8,24,512]{2,1,0:T(8,128)}), f32[8,24,512]{2,1,0:T(8,128)S(1)}, u32[]{:S(2)}, u32[]{:S(2)}) async-start(f32[8,24,512]{2,1,0:T(8,128)} %bitcast.79), calls=%async_computation.12 | async-start | bytes 786432 | tf_op jit(solution)/shard_map/all_to_all | solution.py:18
  13.1 8.0 %all-to-all-done.12 = f32[8,24,512]{2,1,0:T(8,128)S(1)} async-done(((f32[8,24,512]{2,1,0:T(8,128)}), f32[8,24,512]{2,1,0:T(8,128)S(1)}, u32[]{:S(2)}, u32[]{:S(2)}) %all-to-all-start.12) | async-done | bytes 393248 | tf_op jit(solution)/shard_map/all_to_all | solution.py:18
  25.5 14.2 %all-to-all-start.13 = ((f32[16,152,128]{2,1,0:T(8,128)}), f32[16,152,128]{2,1,0:T(8,128)S(1)}, u32[]{:S(2)}, u32[]{:S(2)}) async-start(f32[16,152,128]{2,1,0:T(8,128)} %broadcast_in_dim.113), calls=%async_computation.13 | async-start | bytes 2490368 | tf_op jit(solution)/shard_map/all_to_all | solution.py:18
  40.5 16.3 %all-to-all-done.13.own_ref = f32[16,152,128]{2,1,0:T(8,128)S(1)} async-done(((f32[16,152,128]{2,1,0:T(8,128)}), f32[16,152,128]{2,1,0:T(8,128)S(1)}, u32[]{:S(2)}, u32[]{:S(2)}) %all-to-all-start.13) | async-done | bytes 1245216 | tf_op jit(solution)/shard_map/all_to_all | solution.py:18
  59.5 5.5 %collective-permute-start.21 = (f32[16,152,128]{2,1,0:T(8,128)S(1)}, f32[16,152,128]{2,1,0:T(8,128)S(1)}, u32[]{:S(2)}, u32[]{:S(2)}) collective-permute-start(f32[16,152,128]{2,1,0:T(8,128)S(1)} %all-to-all-done.13.own_ref), channel_id=1, source_target_pairs={{0,64},{64,0},{128,192},{192,128},{256,320},{320,256},{384,448},{4... | collective-permute-start | bytes 3735560 | tf_op jit(solution)/shard_map/ppermute | solution.py:39
  67.5 6.3 %shard_map.40 = f32[1792,128]{1,0:T(8,128)S(1)} custom-call(s32[264]{0:T(512)S(1)} %concatenate.65.info_ref, f32[16,152,128]{2,1,0:T(8,128)S(1)} %all-to-all-done.13.own_ref, f32[16,152,128]{2,1,0:T(8,128)S(1)} %collective-permute-done.21.other_ref), custom_call_target="tpu_custom_call" | custom-call | tf_op jit(solution)/shard_map/pallas_call | solution.py:200
  76.6 6.3 %collective-permute-start.23 = (f32[4,112,128]{2,1,0:T(8,128)S(1)}, f32[4,112,128]{2,1,0:T(8,128)S(1)}, u32[]{:S(2)}, u32[]{:S(2)}) collective-permute-start(f32[4,112,128]{2,1,0:T(8,128)S(1)} %bitcast.274), channel_id=1, source_target_pairs={{0,60},{4,0},{8,4},{12,8},{16,12},{20,16},{24,20},{28,24},{32,28},... | collective-permute-start | bytes 688136 | tf_op jit(solution)/shard_map/ppermute | solution.py:27
  84.9 5.5 %collective-permute-start.25 = (f32[2,112,128]{2,1,0:T(8,128)S(1)}, f32[2,112,128]{2,1,0:T(8,128)S(1)}, u32[]{:S(2)}, u32[]{:S(2)}) collective-permute-start(f32[2,112,128]{2,1,0:T(8,128)S(1)} %bitcast.282), channel_id=1, source_target_pairs={{0,56},{4,60},{8,0},{12,4},{16,8},{20,12},{24,16},{28,20},{32,24},... | collective-permute-start | bytes 344072 | tf_op jit(solution)/shard_map/ppermute | solution.py:27
  94.0 23.4 %all_to_all.106 = f32[4,112,128]{2,1,0:T(8,128)S(1)} all-to-all(f32[4,112,128]{2,1,0:T(8,128)S(1)} %maximum_add_fusion.1), channel_id=1, replica_groups={{0,16,32,48},{4,20,36,52},{8,24,40,56},{12,28,44,60},{1,17,33,49},{5,21..., dimensions={0} | all-to-all | bytes 458752 | tf_op jit(solution)/shard_map/all_to_all | solution.py:18
  117.5 13.9 %all_to_all.107.own_ref = f32[16,112,128]{2,1,0:T(8,128)S(1)} all-to-all(f32[16,112,128]{2,1,0:T(8,128)S(1)} %broadcast_in_dim.121), channel_id=1, replica_groups={{0,1,2,3,128,129,130,131,256,257,258,259,384,385,386,387},{64,65,66,67,..., dimensions={0} | all-to-all | bytes 1835008 | tf_op jit(solution)/shard_map/all_to_all | solution.py:18
  131.4 7.5 %collective-permute-start.26 = (f32[16,112,128]{2,1,0:T(8,128)S(1)}, f32[16,112,128]{2,1,0:T(8,128)S(1)}, u32[]{:S(2)}, u32[]{:S(2)}) collective-permute-start(f32[16,112,128]{2,1,0:T(8,128)S(1)} %all_to_all.107.own_ref), channel_id=1, source_target_pairs={{0,64},{64,0},{128,192},{192,128},{256,320},{320,256},{384,448},{4... | collective-permute-start | bytes 2752520 | tf_op jit(solution)/shard_map/ppermute | solution.py:39
  141.0 6.1 %shard_map.41 = f32[1792,128]{1,0:T(8,128)S(1)} custom-call(s32[256]{0:T(256)S(1)} %concatenate.64.info_ref, f32[16,112,128]{2,1,0:T(8,128)S(1)} %all_to_all.107.own_ref, f32[16,112,128]{2,1,0:T(8,128)S(1)} %collective-permute-done.26.other_ref), custom_call_target="tpu_custom_call" | custom-call | tf_op jit(solution)/shard_map/pallas_call | solution.py:200
  168.1 18.1 %all_to_all.108 = f32[4,112,128]{2,1,0:T(8,128)S(1)} all-to-all(f32[4,112,128]{2,1,0:T(8,128)S(1)} %maximum_add_fusion.2), channel_id=1, replica_groups={{0,16,32,48},{4,20,36,52},{8,24,40,56},{12,28,44,60},{1,17,33,49},{5,21..., dimensions={0} | all-to-all | bytes 458752 | tf_op jit(solution)/shard_map/all_to_all | solution.py:18
  186.3 14.2 %all_to_all.109.own_ref = f32[16,112,128]{2,1,0:T(8,128)S(1)} all-to-all(f32[16,112,128]{2,1,0:T(8,128)S(1)} %broadcast_in_dim.122), channel_id=1, replica_groups={{0,1,2,3,128,129,130,131,256,257,258,259,384,385,386,387},{64,65,66,67,..., dimensions={0} | all-to-all | bytes 1835008 | tf_op jit(solution)/shard_map/all_to_all | solution.py:18
  200.5 9.2 %collective-permute-start.31 = (f32[16,112,128]{2,1,0:T(8,128)S(1)}, f32[16,112,128]{2,1,0:T(8,128)S(1)}, u32[]{:S(2)}, u32[]{:S(2)}) collective-permute-start(f32[16,112,128]{2,1,0:T(8,128)S(1)} %all_to_all.109.own_ref), channel_id=1, source_target_pairs={{0,64},{64,0},{128,192},{192,128},{256,320},{320,256},{384,448},{4... | collective-permute-start | bytes 2752520 | tf_op jit(solution)/shard_map/ppermute | solution.py:39
  211.6 6.1 %shard_map.42 = f32[1792,128]{1,0:T(8,128)S(1)} custom-call(s32[256]{0:T(256)S(1)} %concatenate.63.info_ref, f32[16,112,128]{2,1,0:T(8,128)S(1)} %all_to_all.109.own_ref, f32[16,112,128]{2,1,0:T(8,128)S(1)} %collective-permute-done.31.other_ref), custom_call_target="tpu_custom_call" | custom-call | tf_op jit(solution)/shard_map/pallas_call | solution.py:200
  219.8 6.2 %collective-permute-start.33 = (f32[4,112,128]{2,1,0:T(8,128)S(1)}, f32[4,112,128]{2,1,0:T(8,128)S(1)}, u32[]{:S(2)}, u32[]{:S(2)}) collective-permute-start(f32[4,112,128]{2,1,0:T(8,128)S(1)} %bitcast.276), channel_id=1, source_target_pairs={{0,60},{4,0},{8,4},{12,8},{16,12},{20,16},{24,20},{28,24},{32,28},... | collective-permute-start | bytes 688136 | tf_op jit(solution)/shard_map/ppermute | solution.py:27
  237.7 19.5 %all_to_all.110 = f32[4,112,128]{2,1,0:T(8,128)S(1)} all-to-all(f32[4,112,128]{2,1,0:T(8,128)S(1)} %maximum_add_fusion.3), channel_id=1, replica_groups={{0,16,32,48},{4,20,36,52},{8,24,40,56},{12,28,44,60},{1,17,33,49},{5,21..., dimensions={0} | all-to-all | bytes 458752 | tf_op jit(solution)/shard_map/all_to_all | solution.py:18
  257.3 14.1 %all_to_all.111.own_ref = f32[16,112,128]{2,1,0:T(8,128)S(1)} all-to-all(f32[16,112,128]{2,1,0:T(8,128)S(1)} %broadcast_in_dim.123), channel_id=1, replica_groups={{0,1,2,3,128,129,130,131,256,257,258,259,384,385,386,387},{64,65,66,67,..., dimensions={0} | all-to-all | bytes 1835008 | tf_op jit(solution)/shard_map/all_to_all | solution.py:18
  271.4 8.3 %collective-permute-start.36 = (f32[16,112,128]{2,1,0:T(8,128)S(1)}, f32[16,112,128]{2,1,0:T(8,128)S(1)}, u32[]{:S(2)}, u32[]{:S(2)}) collective-permute-start(f32[16,112,128]{2,1,0:T(8,128)S(1)} %all_to_all.111.own_ref), channel_id=1, source_target_pairs={{0,64},{64,0},{128,192},{192,128},{256,320},{320,256},{384,448},{4... | collective-permute-start | bytes 2752520 | tf_op jit(solution)/shard_map/ppermute | solution.py:39
  281.8 6.5 %shard_map.43 = f32[2304,128]{1,0:T(8,128)S(1)} custom-call(s32[320]{0:T(512)S(1)} %concatenate.61.info_ref, f32[16,112,128]{2,1,0:T(8,128)S(1)} %all_to_all.111.own_ref, f32[16,112,128]{2,1,0:T(8,128)S(1)} %collective-permute-done.36.other_ref), custom_call_target="tpu_custom_call" | custom-call | tf_op jit(solution)/shard_map/pallas_call | solution.py:200
  299.5 5.5 %collective-permute-start.40 = (f32[2,144,128]{2,1,0:T(8,128)S(1)}, f32[2,144,128]{2,1,0:T(8,128)S(1)}, u32[]{:S(2)}, u32[]{:S(2)}) collective-permute-start(f32[2,144,128]{2,1,0:T(8,128)S(1)} %bitcast.280), channel_id=1, source_target_pairs={{0,56},{4,60},{8,0},{12,4},{16,8},{20,12},{24,16},{28,20},{32,24},... | collective-permute-start | bytes 442376 | tf_op jit(solution)/shard_map/ppermute | solution.py:27
  310.7 21.7 %all_to_all.112 = f32[4,144,128]{2,1,0:T(8,128)S(1)} all-to-all(f32[4,144,128]{2,1,0:T(8,128)S(1)} %maximum_add_fusion), channel_id=1, replica_groups={{0,16,32,48},{4,20,36,52},{8,24,40,56},{12,28,44,60},{1,17,33,49},{5,21..., dimensions={0} | all-to-all | bytes 589824 | tf_op jit(solution)/shard_map/all_to_all | solution.py:18
  346.1 7.2 %all-to-all-done.21 = f32[16,16,512]{2,1,0:T(8,128)S(1)} async-done(((f32[16,16,512]{2,1,0:T(8,128)}), f32[16,16,512]{2,1,0:T(8,128)S(1)}, u32[]{:S(2)}, u32[]{:S(2)}) %all-to-all-start.21) | async-done | bytes 524320 | tf_op jit(solution)/shard_map/all_to_all | solution.py:18
  (167 shorter events, 95.7 us)
Async XLA Ops:
  2.8 18.3 %all-to-all-start.12 = ((f32[8,24,512]{2,1,0:T(8,128)}), f32[8,24,512]{2,1,0:T(8,128)S(1)}, u32[]{:S(2)}, u32[]{:S(2)}) async-start(f32[8,24,512]{2,1,0:T(8,128)} %bitcast.79), calls=%async_computation.12 | async-start | bytes 786432 | tf_op jit(solution)/shard_map/all_to_all | solution.py:18
  25.5 31.3 %all-to-all-start.13 = ((f32[16,152,128]{2,1,0:T(8,128)}), f32[16,152,128]{2,1,0:T(8,128)S(1)}, u32[]{:S(2)}, u32[]{:S(2)}) async-start(f32[16,152,128]{2,1,0:T(8,128)} %broadcast_in_dim.113), calls=%async_computation.13 | async-start | bytes 2490368 | tf_op jit(solution)/shard_map/all_to_all | solution.py:18
  59.5 8.0 %collective-permute-start.21 = (f32[16,152,128]{2,1,0:T(8,128)S(1)}, f32[16,152,128]{2,1,0:T(8,128)S(1)}, u32[]{:S(2)}, u32[]{:S(2)}) collective-permute-start(f32[16,152,128]{2,1,0:T(8,128)S(1)} %all-to-all-done.13.own_ref), channel_id=1, source_target_pairs={{0,64},{64,0},{128,192},{192,128},{256,320},{320,256},{384,448},{4... | collective-permute-start | bytes 3735560 | tf_op jit(solution)/shard_map/ppermute | solution.py:39
  73.8 20.1 %collective-permute-start.22 = (f32[4,112,128]{2,1,0:T(8,128)S(1)}, f32[4,112,128]{2,1,0:T(8,128)S(1)}, u32[]{:S(2)}, u32[]{:S(2)}) collective-permute-start(f32[4,112,128]{2,1,0:T(8,128)S(1)} %bitcast.277), channel_id=1, source_target_pairs={{0,4},{4,8},{8,12},{12,16},{16,20},{20,24},{24,28},{28,32},{32,36}... | collective-permute-start | bytes 688136 | tf_op jit(solution)/shard_map/ppermute | solution.py:27
  76.6 17.3 %collective-permute-start.23 = (f32[4,112,128]{2,1,0:T(8,128)S(1)}, f32[4,112,128]{2,1,0:T(8,128)S(1)}, u32[]{:S(2)}, u32[]{:S(2)}) collective-permute-start(f32[4,112,128]{2,1,0:T(8,128)S(1)} %bitcast.274), channel_id=1, source_target_pairs={{0,60},{4,0},{8,4},{12,8},{16,12},{20,16},{24,20},{28,24},{32,28},... | collective-permute-start | bytes 688136 | tf_op jit(solution)/shard_map/ppermute | solution.py:27
  82.9 10.8 %collective-permute-start.24 = (f32[2,112,128]{2,1,0:T(8,128)S(1)}, f32[2,112,128]{2,1,0:T(8,128)S(1)}, u32[]{:S(2)}, u32[]{:S(2)}) collective-permute-start(f32[2,112,128]{2,1,0:T(8,128)S(1)} %bitcast.285), channel_id=1, source_target_pairs={{0,8},{4,12},{8,16},{12,20},{16,24},{20,28},{24,32},{28,36},{32,40... | collective-permute-start | bytes 344072 | tf_op jit(solution)/shard_map/ppermute | solution.py:27
  84.9 9.1 %collective-permute-start.25 = (f32[2,112,128]{2,1,0:T(8,128)S(1)}, f32[2,112,128]{2,1,0:T(8,128)S(1)}, u32[]{:S(2)}, u32[]{:S(2)}) collective-permute-start(f32[2,112,128]{2,1,0:T(8,128)S(1)} %bitcast.282), channel_id=1, source_target_pairs={{0,56},{4,60},{8,0},{12,4},{16,8},{20,12},{24,16},{28,20},{32,24},... | collective-permute-start | bytes 344072 | tf_op jit(solution)/shard_map/ppermute | solution.py:27
  131.4 9.6 %collective-permute-start.26 = (f32[16,112,128]{2,1,0:T(8,128)S(1)}, f32[16,112,128]{2,1,0:T(8,128)S(1)}, u32[]{:S(2)}, u32[]{:S(2)}) collective-permute-start(f32[16,112,128]{2,1,0:T(8,128)S(1)} %all_to_all.107.own_ref), channel_id=1, source_target_pairs={{0,64},{64,0},{128,192},{192,128},{256,320},{320,256},{384,448},{4... | collective-permute-start | bytes 2752520 | tf_op jit(solution)/shard_map/ppermute | solution.py:39
  147.1 20.9 %collective-permute-start.27 = (f32[4,112,128]{2,1,0:T(8,128)S(1)}, f32[4,112,128]{2,1,0:T(8,128)S(1)}, u32[]{:S(2)}, u32[]{:S(2)}) collective-permute-start(f32[4,112,128]{2,1,0:T(8,128)S(1)} %bitcast.278), channel_id=1, source_target_pairs={{0,4},{4,8},{8,12},{12,16},{16,20},{20,24},{24,28},{28,32},{32,36}... | collective-permute-start | bytes 688136 | tf_op jit(solution)/shard_map/ppermute | solution.py:27
  149.1 19.0 %collective-permute-start.28 = (f32[4,112,128]{2,1,0:T(8,128)S(1)}, f32[4,112,128]{2,1,0:T(8,128)S(1)}, u32[]{:S(2)}, u32[]{:S(2)}) collective-permute-start(f32[4,112,128]{2,1,0:T(8,128)S(1)} %bitcast.275), channel_id=1, source_target_pairs={{0,60},{4,0},{8,4},{12,8},{16,12},{20,16},{24,20},{28,24},{32,28},... | collective-permute-start | bytes 688136 | tf_op jit(solution)/shard_map/ppermute | solution.py:27
  153.7 9.4 %collective-permute-start.29 = (f32[2,112,128]{2,1,0:T(8,128)S(1)}, f32[2,112,128]{2,1,0:T(8,128)S(1)}, u32[]{:S(2)}, u32[]{:S(2)}) collective-permute-start(f32[2,112,128]{2,1,0:T(8,128)S(1)} %bitcast.286), channel_id=1, source_target_pairs={{0,8},{4,12},{8,16},{12,20},{16,24},{20,28},{24,32},{28,36},{32,40... | collective-permute-start | bytes 344072 | tf_op jit(solution)/shard_map/ppermute | solution.py:27
  158.0 10.0 %collective-permute-start.30 = (f32[2,112,128]{2,1,0:T(8,128)S(1)}, f32[2,112,128]{2,1,0:T(8,128)S(1)}, u32[]{:S(2)}, u32[]{:S(2)}) collective-permute-start(f32[2,112,128]{2,1,0:T(8,128)S(1)} %bitcast.283), channel_id=1, source_target_pairs={{0,56},{4,60},{8,0},{12,4},{16,8},{20,12},{24,16},{28,20},{32,24},... | collective-permute-start | bytes 344072 | tf_op jit(solution)/shard_map/ppermute | solution.py:27
  200.5 11.1 %collective-permute-start.31 = (f32[16,112,128]{2,1,0:T(8,128)S(1)}, f32[16,112,128]{2,1,0:T(8,128)S(1)}, u32[]{:S(2)}, u32[]{:S(2)}) collective-permute-start(f32[16,112,128]{2,1,0:T(8,128)S(1)} %all_to_all.109.own_ref), channel_id=1, source_target_pairs={{0,64},{64,0},{128,192},{192,128},{256,320},{320,256},{384,448},{4... | collective-permute-start | bytes 2752520 | tf_op jit(solution)/shard_map/ppermute | solution.py:39
  217.8 19.9 %collective-permute-start.32 = (f32[4,112,128]{2,1,0:T(8,128)S(1)}, f32[4,112,128]{2,1,0:T(8,128)S(1)}, u32[]{:S(2)}, u32[]{:S(2)}) collective-permute-start(f32[4,112,128]{2,1,0:T(8,128)S(1)} %bitcast.279), channel_id=1, source_target_pairs={{0,4},{4,8},{8,12},{12,16},{16,20},{20,24},{24,28},{28,32},{32,36}... | collective-permute-start | bytes 688136 | tf_op jit(solution)/shard_map/ppermute | solution.py:27
  219.8 17.9 %collective-permute-start.33 = (f32[4,112,128]{2,1,0:T(8,128)S(1)}, f32[4,112,128]{2,1,0:T(8,128)S(1)}, u32[]{:S(2)}, u32[]{:S(2)}) collective-permute-start(f32[4,112,128]{2,1,0:T(8,128)S(1)} %bitcast.276), channel_id=1, source_target_pairs={{0,60},{4,0},{8,4},{12,8},{16,12},{20,16},{24,20},{28,24},{32,28},... | collective-permute-start | bytes 688136 | tf_op jit(solution)/shard_map/ppermute | solution.py:27
  226.0 9.0 %collective-permute-start.34 = (f32[2,112,128]{2,1,0:T(8,128)S(1)}, f32[2,112,128]{2,1,0:T(8,128)S(1)}, u32[]{:S(2)}, u32[]{:S(2)}) collective-permute-start(f32[2,112,128]{2,1,0:T(8,128)S(1)} %bitcast.287), channel_id=1, source_target_pairs={{0,8},{4,12},{8,16},{12,20},{16,24},{20,28},{24,32},{28,36},{32,40... | collective-permute-start | bytes 344072 | tf_op jit(solution)/shard_map/ppermute | solution.py:27
  228.1 9.6 %collective-permute-start.35 = (f32[2,112,128]{2,1,0:T(8,128)S(1)}, f32[2,112,128]{2,1,0:T(8,128)S(1)}, u32[]{:S(2)}, u32[]{:S(2)}) collective-permute-start(f32[2,112,128]{2,1,0:T(8,128)S(1)} %bitcast.284), channel_id=1, source_target_pairs={{0,56},{4,60},{8,0},{12,4},{16,8},{20,12},{24,16},{28,20},{32,24},... | collective-permute-start | bytes 344072 | tf_op jit(solution)/shard_map/ppermute | solution.py:27
  271.4 10.4 %collective-permute-start.36 = (f32[16,112,128]{2,1,0:T(8,128)S(1)}, f32[16,112,128]{2,1,0:T(8,128)S(1)}, u32[]{:S(2)}, u32[]{:S(2)}) collective-permute-start(f32[16,112,128]{2,1,0:T(8,128)S(1)} %all_to_all.111.own_ref), channel_id=1, source_target_pairs={{0,64},{64,0},{128,192},{192,128},{256,320},{320,256},{384,448},{4... | collective-permute-start | bytes 2752520 | tf_op jit(solution)/shard_map/ppermute | solution.py:39
  288.4 22.3 %collective-permute-start.37 = (f32[4,144,128]{2,1,0:T(8,128)S(1)}, f32[4,144,128]{2,1,0:T(8,128)S(1)}, u32[]{:S(2)}, u32[]{:S(2)}) collective-permute-start(f32[4,144,128]{2,1,0:T(8,128)S(1)} %bitcast.273), channel_id=1, source_target_pairs={{0,4},{4,8},{8,12},{12,16},{16,20},{20,24},{24,28},{28,32},{32,36}... | collective-permute-start | bytes 884744 | tf_op jit(solution)/shard_map/ppermute | solution.py:27
  292.1 18.5 %collective-permute-start.38 = (f32[4,144,128]{2,1,0:T(8,128)S(1)}, f32[4,144,128]{2,1,0:T(8,128)S(1)}, u32[]{:S(2)}, u32[]{:S(2)}) collective-permute-start(f32[4,144,128]{2,1,0:T(8,128)S(1)} %bitcast.272), channel_id=1, source_target_pairs={{0,60},{4,0},{8,4},{12,8},{16,12},{20,16},{24,20},{28,24},{32,28},... | collective-permute-start | bytes 884744 | tf_op jit(solution)/shard_map/ppermute | solution.py:27
  297.5 12.1 %collective-permute-start.39 = (f32[2,144,128]{2,1,0:T(8,128)S(1)}, f32[2,144,128]{2,1,0:T(8,128)S(1)}, u32[]{:S(2)}, u32[]{:S(2)}) collective-permute-start(f32[2,144,128]{2,1,0:T(8,128)S(1)} %bitcast.281), channel_id=1, source_target_pairs={{0,8},{4,12},{8,16},{12,20},{16,24},{20,28},{24,32},{28,36},{32,40... | collective-permute-start | bytes 442376 | tf_op jit(solution)/shard_map/ppermute | solution.py:27
  299.5 11.1 %collective-permute-start.40 = (f32[2,144,128]{2,1,0:T(8,128)S(1)}, f32[2,144,128]{2,1,0:T(8,128)S(1)}, u32[]{:S(2)}, u32[]{:S(2)}) collective-permute-start(f32[2,144,128]{2,1,0:T(8,128)S(1)} %bitcast.280), channel_id=1, source_target_pairs={{0,56},{4,60},{8,0},{12,4},{16,8},{20,12},{24,16},{28,20},{32,24},... | collective-permute-start | bytes 442376 | tf_op jit(solution)/shard_map/ppermute | solution.py:27
  332.4 4.8 %collective-permute-start.41 = (f32[144,128]{1,0:T(8,128)S(1)}, f32[144,128]{1,0:T(8,128)S(1)}, u32[]{:S(2)}, u32[]{:S(2)}) collective-permute-start(f32[144,128]{1,0:T(8,128)S(1)} %reduce_sum.173.own_ref), channel_id=1, source_target_pairs={{0,64},{64,0},{128,192},{192,128},{256,320},{320,256},{384,448},{4... | collective-permute-start | bytes 221192 | tf_op jit(solution)/shard_map/ppermute | solution.py:39
  339.4 13.8 %all-to-all-start.21 = ((f32[16,16,512]{2,1,0:T(8,128)}), f32[16,16,512]{2,1,0:T(8,128)S(1)}, u32[]{:S(2)}, u32[]{:S(2)}) async-start(f32[16,16,512]{2,1,0:T(8,128)} %bitcast.117), calls=%async_computation.21 | async-start | bytes 1048576 | tf_op jit(solution)/shard_map/all_to_all | solution.py:18
  (5 other events, 47.5 us)

commit v3 on v2

--- a/solution.py
+++ b/solution.py
@@ -32,6 +32,15 @@
     far = [[c + 4 * m for m in range(cols // 4)] for c in range(4)]
     near = ahead[0] + shifted(ahead[1], 1) + shifted(ahead[3], -1)
     near = near + jnp.concatenate([shifted(ahead[2][:2], 2), shifted(ahead[2][2:], -2)])
+    return exchange(near, "col", far).sum(0)
+
+
+def sum_slots(pair, up, down):
+    cols = lax.axis_size("col")
+    far = [[c + 4 * m for m in range(cols // 4)] for c in range(4)]
+    two_apart = [[4 * m + b, 4 * m + b + 2] for m in range(cols // 4) for b in range(2)]
+    up, down = shifted(up, 1), shifted(down, -1)
+    near = exchange(pair, "col", two_apart).sum(0) + up + down
     return exchange(near, "col", far).sum(0)
 
 
@@ -236,8 +245,9 @@
     def for_planes(packed):
         packed = packed.reshape(cols // 4, 4, 2, -1)
         packed = lax.dynamic_index_in_dim(packed, core, 2, keepdims=False)
-        twice = jnp.concatenate([packed, packed], axis=1)
-        return lax.dynamic_slice_in_dim(twice, col % 4, 4, 1).transpose(1, 0, 2).reshape(-1)
+        classes = (col % 2, col % 2 + 2, (col + 1) % 4, (col + 3) % 4)
+        parts = [lax.dynamic_index_in_dim(packed, k, 1, keepdims=False) for k in classes]
+        return jnp.concatenate([v.reshape(-1) for v in parts])
 
     part = None
     for step in range(STEPS):
@@ -266,7 +276,8 @@
                 pltpu.VMEM((blocks * LANES, whole), jnp.float32),
             ),
         )(info, own, other)
-        part = sum_along_col(out.reshape(4, cols // 4, slots_out * LANES, TILE))
+        out = out.reshape(4, cols // 4, slots_out * LANES, TILE)
+        part = sum_slots(out[:2], out[2], out[3])
 
     strips = on_core(
         functools.partial(place_kernel, slots=NATURAL, blocks=blocks), (2 * LANES, whole)

time: 361 us -> 369 us (1.022)
  waiting for transfers between devices: 56.9 us -> 71.4 us
  blocking collectives: 125 us -> 117 us
  starting transfers between devices: 126 us -> 121 us
  local copies, waits for them, and re-layouts: 14.1 us -> 18 us
    ppermute x16 -> x8, starting transfers between devices: 62.4 us -> 29.9 us  [shifted(): lax.ppermute(parts, 'col', [(z, (z + by) % cols) for z in range(cols)])]
    all_to_all x3 -> x7, starting transfers between devices: 28 us -> 53.7 us  [exchange(): lax.all_to_all(parts, axis, 0, 0, axis_index_groups=groups, tiled=True)]
    all_to_all x3 -> x7, waiting for transfers between devices: 31.5 us -> 55.3 us  [exchange(): lax.all_to_all(parts, axis, 0, 0, axis_index_groups=groups, tiled=True)]
    ppermute x16 -> x8, waiting for transfers between devices: 20.5 us -> 11.6 us  [shifted(): lax.ppermute(parts, 'col', [(z, (z + by) % cols) for z in range(cols)])]
    all_to_all x7, blocking collectives: 125 us -> 117 us  [exchange(): lax.all_to_all(parts, axis, 0, 0, axis_index_groups=groups, tiled=True)]
  transfers between devices with their start and end apart: 25 -> 21, of which waited for: 16 -> 17; matrix products, arithmetic and copies ran while one was open for 2% -> 2% of each run, Pallas kernels for 0% -> 0%
where the time goes in v3:
time: 369 us; the launch traced here: 362 us
  starting transfers between devices  121 us (33%)
  blocking collectives  117 us (32%)
  waiting for transfers between devices  71.4 us (19%)
  Pallas kernels  26.4 us (7%)
  local copies, waits for them, and re-layouts  18 us (5%)
  other arithmetic  5.54 us (2%)
    all_to_all x7, blocking collectives, exchange(): lax.all_to_all(parts, axis, 0, 0, axis_index_groups=groups, tiled=True)  117 us
    all_to_all x7, waiting for transfers between devices, exchange(): lax.all_to_all(parts, axis, 0, 0, axis_index_groups=groups, tiled=True)  55.3 us
    all_to_all x7, starting transfers between devices, exchange(): lax.all_to_all(parts, axis, 0, 0, axis_index_groups=groups, tiled=True)  53.7 us
    ppermute x5, starting transfers between devices, swap_cores(): lax.ppermute(value, 'row', [(i, i ^ 1) for i in range(lax.axis_size('row'...  36.9 us
    ppermute x8, starting transfers between devices, shifted(): lax.ppermute(parts, 'col', [(z, (z + by) % cols) for z in range(cols)])  29.9 us
    pallas_call x6, Pallas kernels, call(): pl.pallas_call(kernel, out_shape=jax.ShapeDtypeStruct(shape, jnp.float32)...  26.4 us
    ppermute x8, waiting for transfers between devices, shifted(): lax.ppermute(parts, 'col', [(z, (z + by) % cols) for z in range(cols)])  11.6 us
  transfers between devices with their start and end apart: 21, of which 17 were waited for; matrix products, arithmetic and copies ran while one was open for 2% of the time, Pallas kernels for 0%

profile of v3, /device:TPU:1, one launch (start us, length us, event | category | flops | bytes accessed | tf_op | source)
XLA Modules:
  0.0 362.5 jit_solution(8461300573336891318)
XLA Ops:
  2.8 10.2 %all-to-all-start.12 = ((f32[8,24,512]{2,1,0:T(8,128)}), f32[8,24,512]{2,1,0:T(8,128)S(1)}, u32[]{:S(2)}, u32[]{:S(2)}) async-start(f32[8,24,512]{2,1,0:T(8,128)} %bitcast.79), calls=%async_computation.12 | async-start | bytes 786432 | tf_op jit(solution)/shard_map/all_to_all | solution.py:18
  13.1 8.0 %all-to-all-done.12 = f32[8,24,512]{2,1,0:T(8,128)S(1)} async-done(((f32[8,24,512]{2,1,0:T(8,128)}), f32[8,24,512]{2,1,0:T(8,128)S(1)}, u32[]{:S(2)}, u32[]{:S(2)}) %all-to-all-start.12) | async-done | bytes 393248 | tf_op jit(solution)/shard_map/all_to_all | solution.py:18
  25.5 14.2 %all-to-all-start.13 = ((f32[16,152,128]{2,1,0:T(8,128)}), f32[16,152,128]{2,1,0:T(8,128)S(1)}, u32[]{:S(2)}, u32[]{:S(2)}) async-start(f32[16,152,128]{2,1,0:T(8,128)} %broadcast_in_dim.113), calls=%async_computation.13 | async-start | bytes 2490368 | tf_op jit(solution)/shard_map/all_to_all | solution.py:18
  40.6 16.2 %all-to-all-done.13.own_ref = f32[16,152,128]{2,1,0:T(8,128)S(1)} async-done(((f32[16,152,128]{2,1,0:T(8,128)}), f32[16,152,128]{2,1,0:T(8,128)S(1)}, u32[]{:S(2)}, u32[]{:S(2)}) %all-to-all-start.13) | async-done | bytes 1245216 | tf_op jit(solution)/shard_map/all_to_all | solution.py:18
  67.7 6.2 %shard_map.40 = f32[1792,128]{1,0:T(8,128)S(1)} custom-call(s32[264]{0:T(512)S(1)} %concatenate.43.info_ref, f32[16,152,128]{2,1,0:T(8,128)S(1)} %all-to-all-done.13.own_ref, f32[16,152,128]{2,1,0:T(8,128)S(1)} %collective-permute-done.21.other_ref), custom_call_target="tpu_custom_call" | custom-call | tf_op jit(solution)/shard_map/pallas_call | solution.py:209
  80.9 7.6 %collective-permute-start.23 = (f32[4,112,128]{2,1,0:T(8,128)S(1)}, f32[4,112,128]{2,1,0:T(8,128)S(1)}, u32[]{:S(2)}, u32[]{:S(2)}) collective-permute-start(f32[4,112,128]{2,1,0:T(8,128)S(1)} %bitcast.256), channel_id=1, source_target_pairs={{0,60},{4,0},{8,4},{12,8},{16,12},{20,16},{24,20},{28,24},{32,28},... | collective-permute-start | bytes 688136 | tf_op jit(solution)/shard_map/ppermute | solution.py:27
  94.1 23.9 %all_to_all.126 = f32[4,112,128]{2,1,0:T(8,128)S(1)} all-to-all(f32[4,112,128]{2,1,0:T(8,128)S(1)} %add_add_fusion.3), channel_id=1, replica_groups={{0,16,32,48},{4,20,36,52},{8,24,40,56},{12,28,44,60},{1,17,33,49},{5,21..., dimensions={0} | all-to-all | bytes 458752 | tf_op jit(solution)/shard_map/all_to_all | solution.py:18
  118.1 13.5 %all_to_all.127.own_ref = f32[16,112,128]{2,1,0:T(8,128)S(1)} all-to-all(f32[16,112,128]{2,1,0:T(8,128)S(1)} %broadcast_in_dim.121), channel_id=1, replica_groups={{0,1,2,3,128,129,130,131,256,257,258,259,384,385,386,387},{64,65,66,67,..., dimensions={0} | all-to-all | bytes 1835008 | tf_op jit(solution)/shard_map/all_to_all | solution.py:18
  131.6 9.2 %collective-permute-start.24 = (f32[16,112,128]{2,1,0:T(8,128)S(1)}, f32[16,112,128]{2,1,0:T(8,128)S(1)}, u32[]{:S(2)}, u32[]{:S(2)}) collective-permute-start(f32[16,112,128]{2,1,0:T(8,128)S(1)} %all_to_all.127.own_ref), channel_id=1, source_target_pairs={{0,64},{64,0},{128,192},{192,128},{256,320},{320,256},{384,448},{4... | collective-permute-start | bytes 2752520 | tf_op jit(solution)/shard_map/ppermute | solution.py:48
  142.9 6.1 %shard_map.41 = f32[1792,128]{1,0:T(8,128)S(1)} custom-call(s32[256]{0:T(256)S(1)} %concatenate.42.info_ref, f32[16,112,128]{2,1,0:T(8,128)S(1)} %all_to_all.127.own_ref, f32[16,112,128]{2,1,0:T(8,128)S(1)} %collective-permute-done.24.other_ref), custom_call_target="tpu_custom_call" | custom-call | tf_op jit(solution)/shard_map/pallas_call | solution.py:209
  149.8 7.3 %all-to-all-start.17 = ((f32[2,4,112,128]{3,2,1,0:T(8,128)}), f32[2,4,112,128]{3,2,1,0:T(8,128)S(1)}, u32[]{:S(2)}, u32[]{:S(2)}) async-start(f32[2,4,112,128]{3,2,1,0:T(8,128)} %bitcast.94), calls=%async_computation.17 | async-start | bytes 917504 | tf_op jit(solution)/shard_map/all_to_all | solution.py:18
  172.4 16.9 %all_to_all.128 = f32[4,112,128]{2,1,0:T(8,128)S(1)} all-to-all(f32[4,112,128]{2,1,0:T(8,128)S(1)} %add_add_fusion.2), channel_id=1, replica_groups={{0,16,32,48},{4,20,36,52},{8,24,40,56},{12,28,44,60},{1,17,33,49},{5,21..., dimensions={0} | all-to-all | bytes 458752 | tf_op jit(solution)/shard_map/all_to_all | solution.py:18
  189.4 14.0 %all_to_all.129.own_ref = f32[16,112,128]{2,1,0:T(8,128)S(1)} all-to-all(f32[16,112,128]{2,1,0:T(8,128)S(1)} %broadcast_in_dim.122), channel_id=1, replica_groups={{0,1,2,3,128,129,130,131,256,257,258,259,384,385,386,387},{64,65,66,67,..., dimensions={0} | all-to-all | bytes 1835008 | tf_op jit(solution)/shard_map/all_to_all | solution.py:18
  203.4 9.2 %collective-permute-start.27 = (f32[16,112,128]{2,1,0:T(8,128)S(1)}, f32[16,112,128]{2,1,0:T(8,128)S(1)}, u32[]{:S(2)}, u32[]{:S(2)}) collective-permute-start(f32[16,112,128]{2,1,0:T(8,128)S(1)} %all_to_all.129.own_ref), channel_id=1, source_target_pairs={{0,64},{64,0},{128,192},{192,128},{256,320},{320,256},{384,448},{4... | collective-permute-start | bytes 2752520 | tf_op jit(solution)/shard_map/ppermute | solution.py:48
  214.6 6.1 %shard_map.42 = f32[1792,128]{1,0:T(8,128)S(1)} custom-call(s32[256]{0:T(256)S(1)} %concatenate.41.info_ref, f32[16,112,128]{2,1,0:T(8,128)S(1)} %all_to_all.129.own_ref, f32[16,112,128]{2,1,0:T(8,128)S(1)} %collective-permute-done.27.other_ref), custom_call_target="tpu_custom_call" | custom-call | tf_op jit(solution)/shard_map/pallas_call | solution.py:209
  221.5 7.2 %all-to-all-start.20 = ((f32[2,4,112,128]{3,2,1,0:T(8,128)}), f32[2,4,112,128]{3,2,1,0:T(8,128)S(1)}, u32[]{:S(2)}, u32[]{:S(2)}) async-start(f32[2,4,112,128]{3,2,1,0:T(8,128)} %bitcast.97), calls=%async_computation.20 | async-start | bytes 917504 | tf_op jit(solution)/shard_map/all_to_all | solution.py:18
  244.2 16.2 %all_to_all.130 = f32[4,112,128]{2,1,0:T(8,128)S(1)} all-to-all(f32[4,112,128]{2,1,0:T(8,128)S(1)} %add_add_fusion.1), channel_id=1, replica_groups={{0,16,32,48},{4,20,36,52},{8,24,40,56},{12,28,44,60},{1,17,33,49},{5,21..., dimensions={0} | all-to-all | bytes 458752 | tf_op jit(solution)/shard_map/all_to_all | solution.py:18
  260.5 13.9 %all_to_all.131.own_ref = f32[16,112,128]{2,1,0:T(8,128)S(1)} all-to-all(f32[16,112,128]{2,1,0:T(8,128)S(1)} %broadcast_in_dim.123), channel_id=1, replica_groups={{0,1,2,3,128,129,130,131,256,257,258,259,384,385,386,387},{64,65,66,67,..., dimensions={0} | all-to-all | bytes 1835008 | tf_op jit(solution)/shard_map/all_to_all | solution.py:18
  274.5 10.1 %collective-permute-start.30 = (f32[16,112,128]{2,1,0:T(8,128)S(1)}, f32[16,112,128]{2,1,0:T(8,128)S(1)}, u32[]{:S(2)}, u32[]{:S(2)}) collective-permute-start(f32[16,112,128]{2,1,0:T(8,128)S(1)} %all_to_all.131.own_ref), channel_id=1, source_target_pairs={{0,64},{64,0},{128,192},{192,128},{256,320},{320,256},{384,448},{4... | collective-permute-start | bytes 2752520 | tf_op jit(solution)/shard_map/ppermute | solution.py:48
  286.7 6.5 %shard_map.43 = f32[2304,128]{1,0:T(8,128)S(1)} custom-call(s32[320]{0:T(512)S(1)} %concatenate.40.info_ref, f32[16,112,128]{2,1,0:T(8,128)S(1)} %all_to_all.131.own_ref, f32[16,112,128]{2,1,0:T(8,128)S(1)} %collective-permute-done.30.other_ref), custom_call_target="tpu_custom_call" | custom-call | tf_op jit(solution)/shard_map/pallas_call | solution.py:209
  294.0 7.7 %all-to-all-start.23 = ((f32[2,4,144,128]{3,2,1,0:T(8,128)}), f32[2,4,144,128]{3,2,1,0:T(8,128)S(1)}, u32[]{:S(2)}, u32[]{:S(2)}) async-start(f32[2,4,144,128]{3,2,1,0:T(8,128)} %bitcast.100), calls=%async_computation.23 | async-start | bytes 1179648 | tf_op jit(solution)/shard_map/all_to_all | solution.py:18
  308.3 9.1 %all-to-all-done.23 = f32[2,4,144,128]{3,2,1,0:T(8,128)S(1)} async-done(((f32[2,4,144,128]{3,2,1,0:T(8,128)}), f32[2,4,144,128]{3,2,1,0:T(8,128)S(1)}, u32[]{:S(2)}, u32[]{:S(2)}) %all-to-all-start.23) | async-done | bytes 589856 | tf_op jit(solution)/shard_map/all_to_all | solution.py:18
  320.8 18.8 %all_to_all.132 = f32[4,144,128]{2,1,0:T(8,128)S(1)} all-to-all(f32[4,144,128]{2,1,0:T(8,128)S(1)} %add_add_fusion), channel_id=1, replica_groups={{0,16,32,48},{4,20,36,52},{8,24,40,56},{12,28,44,60},{1,17,33,49},{5,21..., dimensions={0} | all-to-all | bytes 589824 | tf_op jit(solution)/shard_map/all_to_all | solution.py:18
  352.2 7.3 %all-to-all-done.25 = f32[16,16,512]{2,1,0:T(8,128)S(1)} async-done(((f32[16,16,512]{2,1,0:T(8,128)}), f32[16,16,512]{2,1,0:T(8,128)S(1)}, u32[]{:S(2)}, u32[]{:S(2)}) %all-to-all-start.25) | async-done | bytes 524320 | tf_op jit(solution)/shard_map/all_to_all | solution.py:18
  (165 shorter events, 96.1 us)
Async XLA Ops:
  2.8 18.3 %all-to-all-start.12 = ((f32[8,24,512]{2,1,0:T(8,128)}), f32[8,24,512]{2,1,0:T(8,128)S(1)}, u32[]{:S(2)}, u32[]{:S(2)}) async-start(f32[8,24,512]{2,1,0:T(8,128)} %bitcast.79), calls=%async_computation.12 | async-start | bytes 786432 | tf_op jit(solution)/shard_map/all_to_all | solution.py:18
  23.0 1.4 collective-permute-start.20
  25.5 14.4 %copy-start.2 = (s32[4]{0:T(128)S(1)}, s32[4]{0:T(128)}, u32[]{:S(2)}) copy-start(s32[4]{0:T(128)} %param.11) | copy-start | bytes 52
  25.5 31.3 %all-to-all-start.13 = ((f32[16,152,128]{2,1,0:T(8,128)}), f32[16,152,128]{2,1,0:T(8,128)S(1)}, u32[]{:S(2)}, u32[]{:S(2)}) async-start(f32[16,152,128]{2,1,0:T(8,128)} %broadcast_in_dim.113), calls=%async_computation.13 | async-start | bytes 2490368 | tf_op jit(solution)/shard_map/all_to_all | solution.py:18
  59.6 8.0 %collective-permute-start.21 = (f32[16,152,128]{2,1,0:T(8,128)S(1)}, f32[16,152,128]{2,1,0:T(8,128)S(1)}, u32[]{:S(2)}, u32[]{:S(2)}) collective-permute-start(f32[16,152,128]{2,1,0:T(8,128)S(1)} %all-to-all-done.13.own_ref), channel_id=1, source_target_pairs={{0,64},{64,0},{128,192},{192,128},{256,320},{320,256},{384,448},{4... | collective-permute-start | bytes 3735560 | tf_op jit(solution)/shard_map/ppermute | solution.py:48
  74.7 16.6 %all-to-all-start.14 = ((f32[2,4,112,128]{3,2,1,0:T(8,128)}), f32[2,4,112,128]{3,2,1,0:T(8,128)S(1)}, u32[]{:S(2)}, u32[]{:S(2)}) async-start(f32[2,4,112,128]{3,2,1,0:T(8,128)} %bitcast.91), calls=%async_computation.14 | async-start | bytes 917504 | tf_op jit(solution)/shard_map/all_to_all | solution.py:18
  78.3 13.7 %collective-permute-start.22 = (f32[4,112,128]{2,1,0:T(8,128)S(1)}, f32[4,112,128]{2,1,0:T(8,128)S(1)}, u32[]{:S(2)}, u32[]{:S(2)}) collective-permute-start(f32[4,112,128]{2,1,0:T(8,128)S(1)} %bitcast.259), channel_id=1, source_target_pairs={{0,4},{4,8},{8,12},{12,16},{16,20},{20,24},{24,28},{28,32},{32,36}... | collective-permute-start | bytes 688136 | tf_op jit(solution)/shard_map/ppermute | solution.py:27
  80.9 13.1 %collective-permute-start.23 = (f32[4,112,128]{2,1,0:T(8,128)S(1)}, f32[4,112,128]{2,1,0:T(8,128)S(1)}, u32[]{:S(2)}, u32[]{:S(2)}) collective-permute-start(f32[4,112,128]{2,1,0:T(8,128)S(1)} %bitcast.256), channel_id=1, source_target_pairs={{0,60},{4,0},{8,4},{12,8},{16,12},{20,16},{24,20},{28,24},{32,28},... | collective-permute-start | bytes 688136 | tf_op jit(solution)/shard_map/ppermute | solution.py:27
  131.6 11.2 %collective-permute-start.24 = (f32[16,112,128]{2,1,0:T(8,128)S(1)}, f32[16,112,128]{2,1,0:T(8,128)S(1)}, u32[]{:S(2)}, u32[]{:S(2)}) collective-permute-start(f32[16,112,128]{2,1,0:T(8,128)S(1)} %all_to_all.127.own_ref), channel_id=1, source_target_pairs={{0,64},{64,0},{128,192},{192,128},{256,320},{320,256},{384,448},{4... | collective-permute-start | bytes 2752520 | tf_op jit(solution)/shard_map/ppermute | solution.py:48
  149.8 19.8 %all-to-all-start.17 = ((f32[2,4,112,128]{3,2,1,0:T(8,128)}), f32[2,4,112,128]{3,2,1,0:T(8,128)S(1)}, u32[]{:S(2)}, u32[]{:S(2)}) async-start(f32[2,4,112,128]{3,2,1,0:T(8,128)} %bitcast.94), calls=%async_computation.17 | async-start | bytes 917504 | tf_op jit(solution)/shard_map/all_to_all | solution.py:18
  157.1 12.6 %collective-permute-start.25 = (f32[4,112,128]{2,1,0:T(8,128)S(1)}, f32[4,112,128]{2,1,0:T(8,128)S(1)}, u32[]{:S(2)}, u32[]{:S(2)}) collective-permute-start(f32[4,112,128]{2,1,0:T(8,128)S(1)} %bitcast.260), channel_id=1, source_target_pairs={{0,4},{4,8},{8,12},{12,16},{16,20},{20,24},{24,28},{28,32},{32,36}... | collective-permute-start | bytes 688136 | tf_op jit(solution)/shard_map/ppermute | solution.py:27
  160.4 12.0 %collective-permute-start.26 = (f32[4,112,128]{2,1,0:T(8,128)S(1)}, f32[4,112,128]{2,1,0:T(8,128)S(1)}, u32[]{:S(2)}, u32[]{:S(2)}) collective-permute-start(f32[4,112,128]{2,1,0:T(8,128)S(1)} %bitcast.257), channel_id=1, source_target_pairs={{0,60},{4,0},{8,4},{12,8},{16,12},{20,16},{24,20},{28,24},{32,28},... | collective-permute-start | bytes 688136 | tf_op jit(solution)/shard_map/ppermute | solution.py:27
  203.4 11.1 %collective-permute-start.27 = (f32[16,112,128]{2,1,0:T(8,128)S(1)}, f32[16,112,128]{2,1,0:T(8,128)S(1)}, u32[]{:S(2)}, u32[]{:S(2)}) collective-permute-start(f32[16,112,128]{2,1,0:T(8,128)S(1)} %all_to_all.129.own_ref), channel_id=1, source_target_pairs={{0,64},{64,0},{128,192},{192,128},{256,320},{320,256},{384,448},{4... | collective-permute-start | bytes 2752520 | tf_op jit(solution)/shard_map/ppermute | solution.py:48
  221.5 19.8 %all-to-all-start.20 = ((f32[2,4,112,128]{3,2,1,0:T(8,128)}), f32[2,4,112,128]{3,2,1,0:T(8,128)S(1)}, u32[]{:S(2)}, u32[]{:S(2)}) async-start(f32[2,4,112,128]{3,2,1,0:T(8,128)} %bitcast.97), calls=%async_computation.20 | async-start | bytes 917504 | tf_op jit(solution)/shard_map/all_to_all | solution.py:18
  228.7 12.6 %collective-permute-start.28 = (f32[4,112,128]{2,1,0:T(8,128)S(1)}, f32[4,112,128]{2,1,0:T(8,128)S(1)}, u32[]{:S(2)}, u32[]{:S(2)}) collective-permute-start(f32[4,112,128]{2,1,0:T(8,128)S(1)} %bitcast.261), channel_id=1, source_target_pairs={{0,4},{4,8},{8,12},{12,16},{16,20},{20,24},{24,28},{28,32},{32,36}... | collective-permute-start | bytes 688136 | tf_op jit(solution)/shard_map/ppermute | solution.py:27
  233.5 10.7 %collective-permute-start.29 = (f32[4,112,128]{2,1,0:T(8,128)S(1)}, f32[4,112,128]{2,1,0:T(8,128)S(1)}, u32[]{:S(2)}, u32[]{:S(2)}) collective-permute-start(f32[4,112,128]{2,1,0:T(8,128)S(1)} %bitcast.258), channel_id=1, source_target_pairs={{0,60},{4,0},{8,4},{12,8},{16,12},{20,16},{24,20},{28,24},{32,28},... | collective-permute-start | bytes 688136 | tf_op jit(solution)/shard_map/ppermute | solution.py:27
  274.5 12.2 %collective-permute-start.30 = (f32[16,112,128]{2,1,0:T(8,128)S(1)}, f32[16,112,128]{2,1,0:T(8,128)S(1)}, u32[]{:S(2)}, u32[]{:S(2)}) collective-permute-start(f32[16,112,128]{2,1,0:T(8,128)S(1)} %all_to_all.131.own_ref), channel_id=1, source_target_pairs={{0,64},{64,0},{128,192},{192,128},{256,320},{320,256},{384,448},{4... | collective-permute-start | bytes 2752520 | tf_op jit(solution)/shard_map/ppermute | solution.py:48
  294.0 23.4 %all-to-all-start.23 = ((f32[2,4,144,128]{3,2,1,0:T(8,128)}), f32[2,4,144,128]{3,2,1,0:T(8,128)S(1)}, u32[]{:S(2)}, u32[]{:S(2)}) async-start(f32[2,4,144,128]{3,2,1,0:T(8,128)} %bitcast.100), calls=%async_computation.23 | async-start | bytes 1179648 | tf_op jit(solution)/shard_map/all_to_all | solution.py:18
  301.8 15.7 %collective-permute-start.31 = (f32[4,144,128]{2,1,0:T(8,128)S(1)}, f32[4,144,128]{2,1,0:T(8,128)S(1)}, u32[]{:S(2)}, u32[]{:S(2)}) collective-permute-start(f32[4,144,128]{2,1,0:T(8,128)S(1)} %bitcast.255), channel_id=1, source_target_pairs={{0,4},{4,8},{8,12},{12,16},{16,20},{20,24},{24,28},{28,32},{32,36}... | collective-permute-start | bytes 884744 | tf_op jit(solution)/shard_map/ppermute | solution.py:27
  303.7 17.0 %collective-permute-start.32 = (f32[4,144,128]{2,1,0:T(8,128)S(1)}, f32[4,144,128]{2,1,0:T(8,128)S(1)}, u32[]{:S(2)}, u32[]{:S(2)}) collective-permute-start(f32[4,144,128]{2,1,0:T(8,128)S(1)} %bitcast.254), channel_id=1, source_target_pairs={{0,60},{4,0},{8,4},{12,8},{16,12},{20,16},{24,20},{28,24},{32,28},... | collective-permute-start | bytes 884744 | tf_op jit(solution)/shard_map/ppermute | solution.py:27
  339.6 3.8 %collective-permute-start.33 = (f32[144,128]{1,0:T(8,128)S(1)}, f32[144,128]{1,0:T(8,128)S(1)}, u32[]{:S(2)}, u32[]{:S(2)}) collective-permute-start(f32[144,128]{1,0:T(8,128)S(1)} %reduce_sum.213.own_ref), channel_id=1, source_target_pairs={{0,64},{64,0},{128,192},{192,128},{256,320},{320,256},{384,448},{4... | collective-permute-start | bytes 221192 | tf_op jit(solution)/shard_map/ppermute | solution.py:48
  344.8 15.6 %copy-start = (f32[512,256]{1,0:T(8,128)S(1)}, f32[512,256]{1,0:T(8,128)}, u32[]{:S(2)}) copy-start(f32[512,256]{1,0:T(8,128)} %param.9) | copy-start | bytes 1572868
  344.8 15.6 %copy-start.3 = (s32[4,2]{0,1:T(2,128)S(1)}, s32[4,2]{0,1:T(2,128)}, u32[]{:S(2)}) copy-start(s32[4,2]{0,1:T(2,128)} %param.10) | copy-start | bytes 100
  345.6 13.9 %all-to-all-start.25 = ((f32[16,16,512]{2,1,0:T(8,128)}), f32[16,16,512]{2,1,0:T(8,128)S(1)}, u32[]{:S(2)}, u32[]{:S(2)}) async-start(f32[16,16,512]{2,1,0:T(8,128)} %bitcast.105), calls=%async_computation.25 | async-start | bytes 1048576 | tf_op jit(solution)/shard_map/all_to_all | solution.py:18
  (1 other events, 0.8 us)
